TPU v7x, 256 devices: a whole 4x4x8 slice. The times are simulated.
256 devices in a mesh: region: 8 (over x, core), dev: 32 (over y, z).
Axes of the slice: x: 4, y: 4, z: 8, core: 2. Of those that a mesh axis runs over, the one named last changes fastest.
Arguments:
- inputs: bfloat16 [49152, 128], P(('region', 'dev')), may hold values from -6 to 6
- responses: bfloat16 [49152], P(('region', 'dev')), may hold values from -6 to 6
- point_slot: int32 [49152], P(('region', 'dev')), may hold values from 0 to 191, as said below
- block_home: int32 [512], replicated, may hold values from 0 to 511, as said below
- nbr_ids: int32 [512, 4], P(('region', 'dev')), may hold values from 0 to 511, as said below
- nbr_count: int32 [512], P(('region', 'dev')), may hold values from 0 to 4, as said below
- w_in: bfloat16 [128, 128], replicated, may hold values from -0.5 to 0.5
- b_in: float32 [128], replicated, may hold values from -3 to 3
- w_out: bfloat16 [128, 128], replicated, may hold values from -0.5 to 0.5
- kernel_params: float32 [3], replicated, may hold values from -1.61 to 2.49, as said below
Outputs:
- block_loglik: float32 [512], P(('region', 'dev'))
- feature_grad: float32 [49152, 128], P(('region', 'dev'))
- grad_w_in: float32 [128, 128], replicated
- grad_b_in: float32 [128], replicated
- grad_w_out: float32 [128, 128], replicated
- grad_kernel: float32 [3], replicated
Inputs may be any that keep to these rules, and one draw needn't show every extreme that they name: `point_slot`: on each device, a permutation of 0 to 2 * 96 - 1 over that device's points. A permutation: block id b is stored in slot block_home[b], on device block_home[b] // 2 in the order region then dev. `nbr_ids`: the first nbr_count[s] entries of row s are distinct ids of blocks whose slots lie in 2 * (s // 2) - 6 to s - 1; the other entries are 0. `nbr_count`: slot 0 has 0; the last slot has 4. `kernel_params`: entry 0 within log(7) to log(12), entry 1 within log(0.5) to log(2), entry 2 within log(0.2) to log(0.6).
All inputs are finite; a program needn't handle non-finite values.
Results may differ from a plain program's by a relative error of at most 0.0097.
Values may be sent and summed in bfloat16 or wider, within the bound.
A program may use at most 64 MiB of HBM per device.

v0:
```python
from functools import partial
import math

import jax
import jax.numpy as jnp
from jax import lax
from jax.sharding import PartitionSpec as P

H = 128
BS = 96
BPD = 2
NMAX = 4
WIN = 3


SQRT_THREE = math.sqrt(3.0)
LOG_TWO_PI = math.log(2.0 * math.pi)


def passed_along(value, axis, steps):
    count = lax.axis_size(axis)
    leading, last = (max(0, -steps), min(count, count - steps))
    return lax.ppermute(value, axis, [(source, source + steps) for source in range(leading, last)])


def block_loglik(resp_joint, valid_rows, joint_rows, params):
    own_rows = joint_rows.shape[0] // (NMAX + 1)
    inv_sq = jnp.exp(-2.0 * params[0])
    variance = jnp.exp(params[1])
    nugget = jnp.exp(params[2])
    sq_norm = jnp.sum(joint_rows * joint_rows, axis=1)
    gram = jnp.dot(joint_rows, joint_rows.T, precision=lax.Precision.HIGHEST)
    dist = jnp.maximum(sq_norm[:, None] + sq_norm[None, :] - 2.0 * gram, 0.0)
    radius = jnp.sqrt(dist * inv_sq + 1e-06)
    kern = variance * (1.0 + SQRT_THREE * radius) * jnp.exp(-SQRT_THREE * radius)
    kmat = kern * valid_rows[:, None] * valid_rows[None, :] + jnp.diag(
        nugget * valid_rows + 1.0 - valid_rows
    )
    factor = jnp.linalg.cholesky(kmat)
    white = lax.linalg.triangular_solve(
        factor, (resp_joint * valid_rows)[:, None], left_side=True, lower=True
    )
    tail = white[-own_rows:, 0]
    diag_tail = jnp.diagonal(factor)[-own_rows:]
    return -0.5 * jnp.sum(tail * tail) - jnp.sum(jnp.log(diag_tail)) - 0.5 * own_rows * LOG_TWO_PI


def network(raw_rows, w_in, b_in, w_out):
    pre = jnp.dot(raw_rows, w_in, preferred_element_type=jnp.float32) + b_in
    hidden = jax.nn.silu(pre).astype(jnp.bfloat16)
    return (
        pre,
        hidden,
        jnp.dot(hidden, w_out, preferred_element_type=jnp.float32).astype(jnp.bfloat16),
    )


def shards(
    inputs, responses, point_slot, block_home, nbr_ids, nbr_count, w_in, b_in, w_out, kernel_params
):
    rows_dev = inputs.shape[0]
    inverse = (
        jnp.zeros((rows_dev,), jnp.int32).at[point_slot].set(jnp.arange(rows_dev, dtype=jnp.int32))
    )
    inputs_slot = inputs[inverse]
    resp_blocks = responses[inverse].reshape(BPD, BS)
    pre_own, hidden_own, feat_own = network(inputs_slot, w_in, b_in, w_out)
    send_main = feat_own.reshape(BPD, BS, H)
    main_parts = []
    resp_parts = []
    for offset in range(1, WIN + 1):
        arrived = passed_along((send_main, resp_blocks), ("region", "dev"), offset)
        main_parts.append(arrived[0])
        resp_parts.append(arrived[1])
    remote_main = jnp.stack(main_parts)
    window_feat = jnp.concatenate([feat_own.reshape(1, BPD, BS, H), remote_main]).reshape(
        (WIN + 1) * BPD, BS, H
    )
    window_resp = jnp.concatenate([resp_blocks[None], jnp.stack(resp_parts)]).reshape(
        (WIN + 1) * BPD, BS
    )
    my_index = lax.axis_index(("region", "dev"))
    nblocks = block_home.shape[0]
    match_table = nbr_ids[:, :, None] == jnp.arange(nblocks, dtype=jnp.int32)[None, None, :]
    nb_slots = jnp.sum(jnp.where(match_table, block_home[None, None, :], 0), axis=2)
    nb_valid = jnp.arange(NMAX, dtype=jnp.int32)[None, :] < nbr_count[:, None]
    nb_flat = jnp.where(nb_valid, (my_index - nb_slots // BPD) * BPD + nb_slots % BPD, 0)
    grad_window = jnp.zeros(((WIN + 1) * BPD, BS, H), jnp.float32)
    hyper_sum = jnp.zeros((3,), jnp.float32)
    loglik_list = []
    for blk_idx in range(BPD):
        slots = jnp.concatenate([nb_flat[blk_idx], jnp.array([blk_idx], jnp.int32)])
        member_mask = jnp.concatenate([nb_valid[blk_idx], jnp.ones((1,), bool)]).astype(jnp.float32)
        joint_rows = (window_feat[slots].astype(jnp.float32) * member_mask[:, None, None]).reshape(
            -1, H
        )
        resp_joint = window_resp[slots].astype(jnp.float32).reshape(-1)
        valid_rows = jnp.repeat(member_mask, BS)
        loglik, pull = jax.vjp(
            partial(block_loglik, resp_joint, valid_rows), joint_rows, kernel_params
        )
        grad_joint, grad_par = pull(jnp.ones((), jnp.float32))
        grad_joint = grad_joint.reshape(NMAX + 1, BS, H) * member_mask[:, None, None]
        grad_window = grad_window.at[slots].add(grad_joint)
        hyper_sum = hyper_sum + grad_par
        loglik_list.append(loglik)
    grad_offsets = grad_window.reshape(WIN + 1, BPD, BS, H)
    total_grad = grad_offsets[0]
    for offset in range(1, WIN + 1):
        total_grad = total_grad + passed_along(grad_offsets[offset], ("region", "dev"), -offset)
    grad_slot = total_grad.reshape(rows_dev, H)
    feature_grad = grad_slot[point_slot]
    part_w_out = jnp.dot(
        hidden_own.astype(jnp.float32).T, grad_slot, precision=lax.Precision.HIGHEST
    )
    back_hidden = jnp.dot(grad_slot, w_out.astype(jnp.float32).T, precision=lax.Precision.HIGHEST)
    sigma = jax.nn.sigmoid(pre_own)
    dpre = back_hidden * sigma * (1.0 + pre_own * (1.0 - sigma))
    part_w_in = jnp.dot(inputs_slot.astype(jnp.float32).T, dpre, precision=lax.Precision.HIGHEST)
    part_b_in = jnp.sum(dpre, axis=0)
    summed = lax.psum((part_w_in, part_b_in, part_w_out, hyper_sum), ("region", "dev"))
    scale = 1.0 / (nblocks * BS)
    block_out = jnp.stack(loglik_list) / BS
    return (
        block_out,
        feature_grad,
        summed[0] * scale,
        summed[1] * scale,
        summed[2] * scale,
        summed[3] * scale,
    )


def solution(mesh):
    placed = (
        P(("region", "dev"), None),
        P(("region", "dev")),
        P(("region", "dev")),
        P(),
        P(("region", "dev"), None),
        P(("region", "dev")),
        P(),
        P(),
        P(),
        P(),
    )
    return jax.shard_map(
        shards,
        mesh=mesh,
        in_specs=placed,
        out_specs=(P(("region", "dev")), P(("region", "dev"), None), P(), P(), P(), P()),
        check_vma=False,
    )
```

profile of v0, /device:TPU:1, one launch (start us, length us, event | category | flops | bytes accessed | tf_op | source)
XLA Modules:
  0.0 906.6 jit_solution(8580562602885976116)
XLA Ops:
  11.4 4.5 collective-permute-start
  15.9 4.9 collective-permute-start.1
  20.8 1.6 gather_fusion.2
  22.4 4.7 collective-permute-start.3
  27.2 3.1 collective-permute-start.4
  30.3 2.4 collective-permute-start.5
  40.6 7.4 collective-permute-start.2
  52.6 2.6 select_add_fusion
  55.8 11.7 %cholesky.368 = f32[128,128]{1,0:T(8,128)S(1)} custom-call(f32[128,128]{1,0:T(8,128)S(1)} %copy.134), custom_call_target="Cholesky" | custom-call | tf_op jit(solution)/shard_map/jvp(jit(cholesky))/cholesky | solution.py:39
  67.6 9.8 %custom-call.50 = f32[1,128,128]{1,2,0:T(8,128)S(1)} custom-call(f32[1,128,128]{2,1,0:T(8,128)S(1)} %get-tuple-element.223), custom_call_target="InvertDiagBlocksLowerTriangular" | custom-call | tf_op jit(solution)/shard_map/jvp(jit(cholesky))/cholesky | solution.py:39
  78.5 11.9 %cholesky.387 = f32[128,128]{1,0:T(8,128)S(1)} custom-call(f32[128,128]{1,0:T(8,128)S(1)} %copy.136), custom_call_target="Cholesky" | custom-call | tf_op jit(solution)/shard_map/jvp(jit(cholesky))/cholesky | solution.py:39
  91.6 9.8 %custom-call.51 = f32[1,128,128]{1,2,0:T(8,128)S(1)} custom-call(f32[1,128,128]{2,1,0:T(8,128)S(1)} %get-tuple-element.220), custom_call_target="InvertDiagBlocksLowerTriangular" | custom-call | tf_op jit(solution)/shard_map/jvp(jit(cholesky))/cholesky | solution.py:39
  102.3 11.7 %cholesky.408 = f32[128,128]{1,0:T(8,128)S(1)} custom-call(f32[128,128]{1,0:T(8,128)S(1)} %copy.138), custom_call_target="Cholesky" | custom-call | tf_op jit(solution)/shard_map/jvp(jit(cholesky))/cholesky | solution.py:39
  114.7 9.8 %custom-call.52 = f32[1,128,128]{1,2,0:T(8,128)S(1)} custom-call(f32[1,128,128]{2,1,0:T(8,128)S(1)} %get-tuple-element.217), custom_call_target="InvertDiagBlocksLowerTriangular" | custom-call | tf_op jit(solution)/shard_map/jvp(jit(cholesky))/cholesky | solution.py:39
  125.3 9.0 cholesky.428
  138.4 6.3 while.13
  139.0 1.4 bitcast_dynamic-update-slice_fusion.9
  141.1 1.4 bitcast_dynamic-update-slice_fusion.9
  143.2 1.4 bitcast_dynamic-update-slice_fusion.9
  146.1 40.1 %custom-call.53 = f32[4,128,128]{1,2,0:T(8,128)S(1)} custom-call(f32[4,128,128]{2,1,0:T(8,128)} %pad_maximum_fusion.5), custom_call_target="InvertDiagBlocksLowerTriangular" | custom-call | tf_op jit(solution)/shard_map/jvp()/triangular_solve/custom-call.9 | solution.py:40
  190.4 4.5 gather_fusion.8
  195.7 26.2 %scatter_fusion.2 = f32[480,480]{1,0:T(8,128)S(1)} fusion(f32[480,480]{1,0:T(8,128)S(1)} %fusion.32, s32[480]{0:T(512)S(1)} %bitcast.446, f32[480]{0:T(512)S(1)} %pad.57), kind=kCustom, calls=%fused_computation.12 | custom fusion | flops 480 | bytes 9600 | tf_op jit(solution)/shard_map/transpose(jvp(jit(diagonal)))/cond/branch_0_fun/scatter-add | solution.py:44
  221.9 2.8 fusion.1
  224.7 5.9 while.15
  225.3 1.3 bitcast_dynamic-update-slice_fusion.11
  227.3 1.3 bitcast_dynamic-update-slice_fusion.11
  231.5 39.7 %custom-call.58 = f32[4,128,128]{1,2,0:T(8,128)S(1)} custom-call(f32[4,128,128]{2,1,0:T(8,128)S(1)} %pad_maximum_fusion.7), custom_call_target="InvertDiagBlocksLowerTriangular" | custom-call | tf_op jit(solution)/shard_map/transpose(jvp(jit(cholesky)))/triangular_solve | solution.py:39
  271.3 1.3 fusion.101
  280.2 1.6 convolution_subtract_fusion.6
  285.0 2.6 select_add_fusion.1
  288.2 11.9 %cholesky.292 = f32[128,128]{1,0:T(8,128)S(1)} custom-call(f32[128,128]{1,0:T(8,128)S(1)} %copy.117), custom_call_target="Cholesky" | custom-call | tf_op jit(solution)/shard_map/jvp(jit(cholesky))/cholesky | solution.py:39
  300.2 9.8 %custom-call.45 = f32[1,128,128]{1,2,0:T(8,128)S(1)} custom-call(f32[1,128,128]{2,1,0:T(8,128)S(1)} %get-tuple-element.215), custom_call_target="InvertDiagBlocksLowerTriangular" | custom-call | tf_op jit(solution)/shard_map/jvp(jit(cholesky))/cholesky | solution.py:39
  310.9 11.7 %cholesky.311 = f32[128,128]{1,0:T(8,128)S(1)} custom-call(f32[128,128]{1,0:T(8,128)S(1)} %copy.119), custom_call_target="Cholesky" | custom-call | tf_op jit(solution)/shard_map/jvp(jit(cholesky))/cholesky | solution.py:39
  323.0 9.8 %custom-call.46 = f32[1,128,128]{1,2,0:T(8,128)S(1)} custom-call(f32[1,128,128]{2,1,0:T(8,128)S(1)} %get-tuple-element.213), custom_call_target="InvertDiagBlocksLowerTriangular" | custom-call | tf_op jit(solution)/shard_map/jvp(jit(cholesky))/cholesky | solution.py:39
  333.8 12.1 %cholesky.332 = f32[128,128]{1,0:T(8,128)S(1)} custom-call(f32[128,128]{1,0:T(8,128)S(1)} %copy.125), custom_call_target="Cholesky" | custom-call | tf_op jit(solution)/shard_map/jvp(jit(cholesky))/cholesky | solution.py:39
  346.1 9.8 %custom-call.47 = f32[1,128,128]{1,2,0:T(8,128)S(1)} custom-call(f32[1,128,128]{2,1,0:T(8,128)S(1)} %get-tuple-element.211), custom_call_target="InvertDiagBlocksLowerTriangular" | custom-call | tf_op jit(solution)/shard_map/jvp(jit(cholesky))/cholesky | solution.py:39
  356.8 8.8 cholesky.352
  372.8 9.1 %while.12 = (s32[]{:T(128)}, f32[480,480]{0,1:T(8,128)}, s32[3,2]{0,1:T(2,128)S(1)}, f32[3,128,128]{2,1,0:T(8,128)S(1)}, s32[]{:T(128)}) while((s32[]{:T(128)}, f32[480,480]{0,1:T(8,128)}, s32[3,2]{0,1:T(2,128)S(1)}, f32[3,128,128]{2,1,0:T(8,128)S(1)}, s32[]{:T(128)}) %tuple.163), condition=%wide.while_cond, body=%wide.while_body.sunk | while | flops 2 | bytes 393321 | solution.py:40
  373.4 2.3 dynamic-slice.30
  376.4 2.3 dynamic-slice.30
  379.4 2.3 dynamic-slice.30
  382.0 39.3 %custom-call.48 = f32[4,128,128]{1,2,0:T(8,128)S(1)} custom-call(f32[4,128,128]{2,1,0:T(8,128)S(1)} %pad_maximum_fusion.4), custom_call_target="InvertDiagBlocksLowerTriangular" | custom-call | tf_op jit(solution)/shard_map/jvp()/triangular_solve/custom-call.9 | solution.py:40
  426.1 4.5 gather_fusion.7
  430.6 6.4 while.14
  431.3 1.4 dynamic-slice.34
  433.4 1.4 dynamic-slice.34
  435.5 1.4 dynamic-slice.34
  437.1 39.9 %custom-call.56 = f32[4,128,128]{1,2,0:T(8,128)} custom-call(f32[4,128,128]{2,1,0:T(8,128)S(1)} %pad_maximum_fusion.6), custom_call_target="InvertDiagBlocksLowerTriangular" | custom-call | tf_op jit(solution)/shard_map/transpose(jvp(jit(cholesky)))/triangular_solve | solution.py:39
  482.0 26.4 %scatter_fusion = f32[480,480]{1,0:T(8,128)S(1)} fusion(f32[480,480]{1,0:T(8,128)S(1)} %fusion.31, s32[480]{0:T(512)S(1)} %bitcast.447, f32[480]{0:T(512)S(1)} %pad.55), kind=kCustom, calls=%fused_computation.10 | custom fusion | flops 480 | bytes 9600 | tf_op jit(solution)/shard_map/transpose(jvp(jit(diagonal)))/cond/branch_0_fun/scatter-add | solution.py:44
  509.6 3.0 fusion.3
  519.8 1.8 fusion.103
  528.4 4.0 select_reduce_fusion
  535.3 1.4 convolution_subtract_fusion.5
  542.1 4.1 select_reduce_fusion.1
  548.9 1.6 fusion.253
  551.5 1.8 fusion.7
  555.4 1.8 fusion.9
  559.6 3.8 collective-permute-start.6
  563.4 5.4 collective-permute-start.7
  568.7 6.4 collective-permute-start.8
  580.5 78.6 %all-reduce.17 = (f32[128]{0:T(128)S(1)}, f32[3]{0:T(128)S(1)}) all-reduce(f32[128]{0:T(128)S(1)} %get-tuple-element.249, f32[3]{0:T(128)S(1)} %add_add_fusion), channel_id=1, replica_groups=mesh['region'=8,'dev'=32] {'region','dev'}, use_global_device_ids=true, to_apply=%region_26.32 | all-reduce | flops 131 | bytes 1048 | tf_op jit(solution)/shard_map/psum | solution.py:121
  661.1 1.4 gather_fusion.6
  662.5 234.9 %all-reduce.21.cloned.1.call-done = (f32[128,128]{1,0:T(8,128)}, f32[128,128]{1,0:T(8,128)}) async-done(((f32[128,128]{1,0:T(8,128)}, f32[128,128]{1,0:T(8,128)}), (f32[128,128]{1,0:T(8,128)}, f32[128,128]{1,0:T(8,128)})) %all-reduce.21.cloned.1.call-update) | async-done | bytes 131088 | tf_op jit(solution)/shard_map/psum | solution.py:121
  897.4 1.5 broadcast_multiply_fusion.4
  (366 shorter events, 99.6 us)
Async XLA Ops:
  7.2 2.0 copy-start
  7.2 890.2 %all-reduce.21.cloned.1.call-start = ((), (), s32[]{:S(2)}) async-start(), calls=%async_computation | async-start | bytes 262144 | tf_op jit(solution)/shard_map/psum | solution.py:121
  9.1 0.8 copy-start.27
  9.2 0.8 copy-start.39
  10.0 0.8 copy-start.41
  10.7 0.6 copy-start.24
  11.4 9.4 %copy-start.1 = (bf16[192]{0:T(256)(128)(2,1)S(1)}, bf16[192]{0:T(256)(128)(2,1)}, u32[]{:S(2)}) copy-start(bf16[192]{0:T(256)(128)(2,1)} %param.26) | copy-start | bytes 1156
  11.4 39.3 %collective-permute-start = (bf16[2,96,128]{2,1,0:T(8,128)(2,1)S(1)}, bf16[2,96,128]{2,1,0:T(8,128)(2,1)S(1)}, u32[]{:S(2)}, u32[]{:S(2)}) collective-permute-start(bf16[2,96,128]{2,1,0:T(8,128)(2,1)S(1)} %bitcast.461), channel_id=1, source_target_pairs={{0,1},{1,2},{2,3},{3,4},{4,5},{5,6},{6,7},{7,8},{8,9},{9,10},{10,1... | collective-permute-start | bytes 147464 | tf_op jit(solution)/shard_map/ppermute | solution.py:23
  15.9 34.8 %collective-permute-start.1 = (bf16[2,96,128]{2,1,0:T(8,128)(2,1)S(1)}, bf16[2,96,128]{2,1,0:T(8,128)(2,1)S(1)}, u32[]{:S(2)}, u32[]{:S(2)}) collective-permute-start(bf16[2,96,128]{2,1,0:T(8,128)(2,1)S(1)} %bitcast.462), channel_id=1, source_target_pairs={{0,2},{1,3},{2,4},{3,5},{4,6},{5,7},{6,8},{7,9},{8,10},{9,11},{10,... | collective-permute-start | bytes 147464 | tf_op jit(solution)/shard_map/ppermute | solution.py:23
  22.4 18.1 %collective-permute-start.3 = (bf16[2,96]{1,0:T(2,128)(2,1)S(1)}, bf16[2,96]{1,0:T(2,128)(2,1)S(1)}, u32[]{:S(2)}, u32[]{:S(2)}) collective-permute-start(bf16[2,96]{1,0:T(2,128)(2,1)S(1)} %reshape.658), channel_id=1, source_target_pairs={{0,1},{1,2},{2,3},{3,4},{4,5},{5,6},{6,7},{7,8},{8,9},{9,10},{10,1... | collective-permute-start | bytes 1160 | tf_op jit(solution)/shard_map/ppermute | solution.py:23
  27.2 20.8 %collective-permute-start.4 = (bf16[2,96]{1,0:T(2,128)(2,1)S(1)}, bf16[2,96]{1,0:T(2,128)(2,1)S(1)}, u32[]{:S(2)}, u32[]{:S(2)}) collective-permute-start(bf16[2,96]{1,0:T(2,128)(2,1)S(1)} %reshape.658), channel_id=1, source_target_pairs={{0,2},{1,3},{2,4},{3,5},{4,6},{5,7},{6,8},{7,9},{8,10},{9,11},{10,... | collective-permute-start | bytes 1160 | tf_op jit(solution)/shard_map/ppermute | solution.py:23
  30.3 17.7 %collective-permute-start.5 = (bf16[2,96]{1,0:T(2,128)(2,1)S(1)}, bf16[2,96]{1,0:T(2,128)(2,1)S(1)}, u32[]{:S(2)}, u32[]{:S(2)}) collective-permute-start(bf16[2,96]{1,0:T(2,128)(2,1)S(1)} %reshape.658), channel_id=1, source_target_pairs={{0,3},{1,4},{2,5},{3,6},{4,7},{5,8},{6,9},{7,10},{8,11},{9,12},{10... | collective-permute-start | bytes 1160 | tf_op jit(solution)/shard_map/ppermute | solution.py:23
  34.0 0.7 copy-start.40
  34.7 0.7 copy-start.36
  34.7 0.7 copy-start.38
  35.8 0.6 copy-start.31
  35.8 2.6 copy-start.33
  36.4 0.7 copy-start.35
  38.4 10.3 %copy-start.30 = (s32[1024]{0:T(1024)}, s32[1024]{0:T(1024)S(1)}, u32[]{:S(2)}) copy-start(s32[1024]{0:T(1024)S(1)} %pad_clamp_fusion.2) | copy-start | bytes 12292
  40.6 10.7 %collective-permute-start.2 = (bf16[2,96,128]{2,1,0:T(8,128)(2,1)S(1)}, bf16[2,96,128]{2,1,0:T(8,128)(2,1)S(1)}, u32[]{:S(2)}, u32[]{:S(2)}) collective-permute-start(bf16[2,96,128]{2,1,0:T(8,128)(2,1)S(1)} %bitcast.463), channel_id=1, source_target_pairs={{0,3},{1,4},{2,5},{3,6},{4,7},{5,8},{6,9},{7,10},{8,11},{9,12},{10... | collective-permute-start | bytes 147464 | tf_op jit(solution)/shard_map/ppermute | solution.py:23
  51.3 0.8 copy-start.17
  51.9 0.6 copy-start.12
  137.7 0.7 copy-start.43
  186.2 0.8 copy-start.29
  224.7 47.9 %copy-start.19 = (f32[480,480]{1,0:T(8,128)S(1)}, f32[480,480]{1,0:T(8,128)}, u32[]{:S(2)}) copy-start(f32[480,480]{1,0:T(8,128)} %fusion.1) | copy-start | bytes 2764804
  271.2 4.7 copy-start.20
  276.5 1.0 copy-start.21
  281.9 0.9 copy-start.18
  283.6 0.6 copy-start.14
  284.3 0.7 copy-start.37
  381.8 39.5 %copy-start.28 = (f32[480,1]{0,1:T(1,128)S(1)}, f32[480,1]{0,1:T(1,128)}, u32[]{:S(2)}) copy-start(f32[480,1]{0,1:T(1,128)} %mul.425) | copy-start | bytes 5764
  514.4 1.0 copy-start.22
  519.8 1.9 copy-start.13
  521.6 0.9 copy-start.15
  522.5 0.9 copy-start.16
  523.5 2.0 copy-start.7
  524.8 0.7 copy-start.8
  527.2 1.3 copy-start.2
  528.4 6.7 copy-start.11
  532.5 4.8 copy-start.6
  535.3 1.4 copy-start.23
  540.8 1.3 copy-start.4
  542.1 6.8 copy-start.3
  548.9 1.6 copy-start.10
  551.5 1.9 copy-start.5
  553.5 0.9 copy-start.9
  557.3 0.6 copy-start.34
  557.8 0.8 copy-start.32
  559.6 18.9 %collective-permute-start.6 = (f32[2,96,128]{2,1,0:T(8,128)S(1)}, f32[2,96,128]{2,1,0:T(8,128)S(1)}, u32[]{:S(2)}, u32[]{:S(2)}) collective-permute-start(f32[2,96,128]{2,1,0:T(8,128)S(1)} %get-tuple-element.201), channel_id=1, source_target_pairs={{1,0},{2,1},{3,2},{4,3},{5,4},{6,5},{7,6},{8,7},{9,8},{10,9},{11,1... | collective-permute-start | bytes 294920 | tf_op jit(solution)/shard_map/ppermute | solution.py:23
  563.4 15.1 %collective-permute-start.7 = (f32[2,96,128]{2,1,0:T(8,128)S(1)}, f32[2,96,128]{2,1,0:T(8,128)S(1)}, u32[]{:S(2)}, u32[]{:S(2)}) collective-permute-start(f32[2,96,128]{2,1,0:T(8,128)S(1)} %get-tuple-element.203), channel_id=1, source_target_pairs={{2,0},{3,1},{4,2},{5,3},{6,4},{7,5},{8,6},{9,7},{10,8},{11,9},{12,... | collective-permute-start | bytes 294920 | tf_op jit(solution)/shard_map/ppermute | solution.py:23
  568.7 10.1 %collective-permute-start.8 = (f32[2,96,128]{2,1,0:T(8,128)S(1)}, f32[2,96,128]{2,1,0:T(8,128)S(1)}, u32[]{:S(2)}, u32[]{:S(2)}) collective-permute-start(f32[2,96,128]{2,1,0:T(8,128)S(1)} %get-tuple-element.202), channel_id=1, source_target_pairs={{3,0},{4,1},{5,2},{6,3},{7,4},{8,5},{9,6},{10,7},{11,8},{12,9},{13... | collective-permute-start | bytes 294920 | tf_op jit(solution)/shard_map/ppermute | solution.py:23
  578.4 0.9 copy-start.25
  578.4 0.9 copy-start.42
  897.4 1.5 copy-start.26
Sparse Core Ops, SparseCore 0:
  660.7 236.6 all-reduce.20
where the time goes:
time: 911 us; the launch traced here: 907 us
  other arithmetic  396 us (43%)
  waiting for transfers between devices  236 us (26%)
  blocking collectives  78.6 us (9%)
  local copies, waits for them, and re-layouts  65.7 us (7%)
  matrix products  58.2 us (6%)
  starting transfers between devices  42.7 us (5%)
  between operations  29.3 us (3%)
    another operation x40, other arithmetic, block_loglik(): factor = jnp.linalg.cholesky(kmat)  236 us
    psum x1, waiting for transfers between devices, shards(): lax.psum((part_w_in, part_b_in, part_w_out, hyper_sum), ('region', 'dev'))  235 us
    another operation x15, other arithmetic, block_loglik(): lax.linalg.triangular_solve(factor, (resp_joint * valid_rows)[:, None], l...  82.4 us
    psum x1, blocking collectives, shards(): lax.psum((part_w_in, part_b_in, part_w_out, hyper_sum), ('region', 'dev'))  78.6 us
    scatter-add x2, other arithmetic, block_loglik(): diag_tail = jnp.diagonal(factor)[-own_rows:]  52.6 us
    ppermute x9, starting transfers between devices, passed_along(): lax.ppermute(value, axis, [(source, source + steps) for source in range(l...  42.6 us
    another operation x40, matrix products, block_loglik(): factor = jnp.linalg.cholesky(kmat)  26.6 us
  transfers between devices with their start and end apart: 10, of which 3 were waited for; matrix products, arithmetic and copies ran while one was open for 1% of the time, Pallas kernels for 0%

commit v1 on v0

v1 whole, which is shorter than its diff:
```python
import math

import jax
import jax.numpy as jnp
from jax import lax
from jax.experimental import pallas as pl
from jax.experimental.pallas import tpu as pltpu
from jax.sharding import PartitionSpec as P

H = 128
BS = 96
BPD = 2
NMAX = 4
WIN = 3
ROWS = BPD * BS
B = 128
N = 4 * B
STEPS = 7

SQRT_THREE = math.sqrt(3.0)
LOG_TWO_PI = math.log(2.0 * math.pi)
MESH = pl.DeviceIdType.MESH
F32 = jnp.float32
BF16 = jnp.bfloat16


def dot(a, b, contract=((1,), (0,))):
    return lax.dot_general(a, b, (contract, ((), ())), preferred_element_type=F32)


NT = ((1,), (1,))
TN = ((0,), (0,))


def split2(a):
    hi = a.astype(BF16)
    return hi, (a - hi.astype(F32)).astype(BF16)


def split3(a):
    hi = a.astype(BF16)
    rest = a - hi.astype(F32)
    mid = rest.astype(BF16)
    return hi, mid, (rest - mid.astype(F32)).astype(BF16)


def wide(parts, cols):
    row = jnp.concatenate(parts, axis=1)
    return jnp.concatenate([row, row], axis=0)


def mul2(a, b):
    n = b.shape[1]
    out = dot(jnp.concatenate(split2(a), axis=1), wide(split2(b), n))
    return out[:, :n] + out[:, n:]


def mul3(a, b):
    n = b.shape[1]
    ah, am, al = split3(a)
    bh, bm, bl = split3(b)
    out = dot(jnp.concatenate([ah, am], axis=1), wide((bh, bm), n))
    low = dot(jnp.concatenate([ah, al], axis=1), jnp.concatenate([bl, bh], axis=0))
    return out[:, :n] + (out[:, n:] + low)


def eye_of(n):
    return (
        lax.broadcasted_iota(jnp.int32, (n, n), 0) == lax.broadcasted_iota(jnp.int32, (n, n), 1)
    ).astype(F32)


def inverses(mats, eye, coef, scales):
    res = [eye - coef * a for a in mats]
    inv = [(scales[0] * coef) * (eye + r) for r in res]
    res = [(1.0 - scales[0]) * eye + scales[0] * mul2(r, r) for r in res]
    for j in range(1, STEPS):
        s = scales[j]
        if j < STEPS - 1:
            both = [mul2(jnp.concatenate([x, r], axis=0), r) for x, r in zip(inv, res)]
            inv = [s * (x + b[:B]) for x, b in zip(inv, both)]
            res = [(1.0 - s) * eye + s * b[B:] for b in both]
        else:
            inv = [s * (x + mul2(x, r)) for x, r in zip(inv, res)]
    left = [eye - mul3(a, x) for a, x in zip(mats, inv)]
    return [x + mul2(x, t) for x, t in zip(inv, left)]


def device(index):
    per = lax.axis_size("dev")
    return (index // per, index % per)


def my_index():
    return lax.axis_index("region") * lax.axis_size("dev") + lax.axis_index("dev")


def network(x, w_in, b_in, w_out):
    pre = dot(x, w_in) + b_in
    sig = 1.0 / (1.0 + jnp.exp(-pre))
    hidden = (pre * sig).astype(BF16)
    return pre, sig, hidden


def one_hot(point_slot, rows, first):
    slot = lax.broadcasted_iota(jnp.int32, (rows, ROWS), 0) + first
    return (slot == point_slot).astype(F32).astype(BF16)


def send_kernel(x_ref, resp_ref, ps_ref, w_in_ref, b_ref, w_out_ref, win_ref, send_sem, recv_sem):
    total = lax.axis_size("region") * lax.axis_size("dev")
    me = my_index()
    barrier = pltpu.get_barrier_semaphore()
    for k in range(1, WIN + 1):
        pl.semaphore_signal(
            barrier, inc=1, device_id=device(lax.rem(me + total - k, total)), device_id_type=MESH
        )
    _, _, hidden = network(x_ref[...], w_in_ref[...], b_ref[...], w_out_ref[...])
    feats = dot(hidden, w_out_ref[...]).astype(BF16)
    point_slot = ps_ref[...]
    win_ref[0, :ROWS, :] = dot(one_hot(point_slot, ROWS, 0), feats).astype(BF16)
    resp = jnp.broadcast_to(resp_ref[...].astype(F32), (16, ROWS)).astype(BF16)
    first = dot(resp, one_hot(point_slot, B, 0), NT)
    second = dot(resp, one_hot(point_slot, B, BS), NT)
    half = lax.broadcasted_iota(jnp.int32, (16, B), 0) < 8
    win_ref[0, ROWS:, :] = jnp.where(half, first, second).astype(BF16)
    pl.semaphore_wait(barrier, WIN)
    copies = []
    for k in range(1, WIN + 1):
        copies.append(
            pltpu.make_async_remote_copy(
                src_ref=win_ref.at[0],
                dst_ref=win_ref.at[k],
                send_sem=send_sem.at[k - 1],
                recv_sem=recv_sem.at[k - 1],
                device_id=device(lax.rem(me + k, total)),
                device_id_type=MESH,
            )
        )
        copies[-1].start()
    for c in copies:
        c.wait()


def block_kernel(
    home_ref, ids_ref, cnt_ref, par_ref, win_ref, ll_ref, hyp_ref, gw_ref, z_ref, e_ref, k_ref
):
    me = my_index()

    def const(x):
        return jnp.full((1, 1), x, F32)

    inv_sq = jnp.exp(-2.0 * const(par_ref[0]))
    var = jnp.exp(const(par_ref[1]))
    nug = jnp.exp(const(par_ref[2]))
    eye = eye_of(B)
    lane = lax.broadcasted_iota(jnp.int32, (B, B), 1)
    sub = lax.broadcasted_iota(jnp.int32, (B, B), 0)
    pick = (lane == BS).astype(F32).astype(BF16)

    top = B * var + 1.0
    coef = 2.0 / (top + nug)
    delta = (top - nug) / (top + nug)
    scales = []
    for _ in range(STEPS):
        sq = delta * delta
        scales.append(2.0 / (2.0 - sq))
        delta = sq / (2.0 - sq)

    wins = []
    for s in range(BPD):
        count = cnt_ref[s]
        row_wins = []
        resp_rows = []
        for k in range(NMAX + 1):
            if k < NMAX:
                slot = home_ref[ids_ref[s, k]]
                live = k < count
                w = jnp.where(live, (me - slot // BPD) * BPD + slot % BPD, 0)
                w = jnp.clip(w, 0, (WIN + 1) * BPD - 1)
                flag = jnp.where(live, 1.0, 0.0)
            else:
                w = jnp.int32(s)
                flag = jnp.float32(1.0)
            row_wins.append(w)
            member = win_ref[w // BPD, pl.ds(pl.multiple_of((w % BPD) * BS, BS), BS), :]
            z_ref[s, k * BS : (k + 1) * BS, :] = (member.astype(F32) * flag).astype(BF16)
            tile = win_ref[w // BPD, ROWS : ROWS + 16, :].astype(F32)
            resp = jnp.where(w % BPD == 0, tile[0:1], tile[8:9]) * flag
            resp_rows.append(jnp.where(eye[:BS] > 0.0, resp, 0.0).astype(BF16))
        z_ref[s, (NMAX + 1) * BS :, :] = jnp.zeros((N - (NMAX + 1) * BS, B), BF16)
        resp_rows.append(jnp.zeros((N - (NMAX + 1) * BS, B), BF16))
        wins.append(row_wins)
        resp_col = dot(jnp.concatenate(resp_rows, axis=0), pick)

        z = z_ref[s]
        gram = dot(z, z, NT)
        diag = [jnp.where(eye > 0.0, gram[i * B : (i + 1) * B, i * B : (i + 1) * B], 0.0) for i in range(4)]
        sq_row = jnp.concatenate([jnp.sum(d, axis=0, keepdims=True) for d in diag], axis=1)
        col_id = lax.broadcasted_iota(jnp.int32, (1, N), 1)
        own = (col_id >= NMAX * BS) & (col_id < (NMAX + 1) * BS)
        v_row = jnp.where((col_id < count * BS) | own, 1.0, 0.0)
        for i in range(4):
            rows = slice(i * B, (i + 1) * B)
            row_id = lax.broadcasted_iota(jnp.int32, (B, 1), 0) + i * B
            own_c = (row_id >= NMAX * BS) & (row_id < (NMAX + 1) * BS)
            v_col = jnp.where((row_id < count * BS) | own_c, 1.0, 0.0)
            sq_col = jnp.sum(diag[i], axis=1, keepdims=True)
            for c in range(0, B, 32):
                part = slice(c, c + 32)
                d2 = jnp.maximum(sq_col[part] + sq_row - 2.0 * gram[i * B + c : i * B + c + 32], 0.0)
                r2 = d2 * inv_sq + 1e-06
                rad = SQRT_THREE * (r2 * lax.rsqrt(r2))
                e = jnp.exp(-rad) * (v_col[part] * v_row)
                e_ref[s, i * B + c : i * B + c + 32, :] = e
                on = lax.broadcasted_iota(jnp.int32, (32, N), 0) + (i * B + c) == lax.broadcasted_iota(
                    jnp.int32, (32, N), 1
                )
                k = var * (1.0 + rad) * e + jnp.where(on, nug * v_col[part] + 1.0 - v_col[part], 0.0)
                k_ref[s, i * B + c : i * B + c + 32, :] = k
            k_ref[s, rows, 3 * B :] = k_ref[s, rows, 3 * B :] + resp_col[rows]

    both = range(BPD)
    invs = []
    for i in range(3):
        lo = (i + 1) * B
        rows = slice(i * B, lo)
        cur = inverses([k_ref[s, rows, rows] for s in both], eye, coef, scales)
        invs.append(cur)
        for s in both:
            panel = mul3(k_ref[s, lo:, rows], cur[s])
            k_ref[s, lo:, lo:] = k_ref[s, lo:, lo:] - mul3(panel, k_ref[s, rows, lo:])
    real = (lane < BS) & (sub < BS)
    resid = [jnp.where((sub < BS) & (lane == BS), k_ref[s, 3 * B :, 3 * B :], 0.0) for s in both]
    schur = [jnp.where(real, k_ref[s, 3 * B :, 3 * B :], eye) for s in both]
    s_inv = inverses(schur, eye, coef, scales)

    hyper = jnp.zeros((1, B), F32)
    lane1 = lax.broadcasted_iota(jnp.int32, (1, B), 1)
    gw_ref[...] = jnp.zeros_like(gw_ref)
    for s in both:
        x3 = mul3(invs[2][s], k_ref[s, 2 * B : 3 * B, 3 * B :])
        x2 = mul3(invs[1][s], k_ref[s, B : 2 * B, 3 * B :] - mul3(k_ref[s, B : 2 * B, 2 * B : 3 * B], x3))
        t1 = k_ref[s, :B, 3 * B :] - mul3(k_ref[s, :B, B : 2 * B], x2) - mul3(k_ref[s, :B, 2 * B : 3 * B], x3)
        x1 = mul3(invs[0][s], t1)
        beta = mul3(s_inv[s], resid[s])
        beta_t = beta.T
        beta_col = jnp.sum(beta, axis=1, keepdims=True)
        beta_row = jnp.sum(beta_t, axis=0, keepdims=True)
        mid = jnp.where(real, beta_col * beta_row - s_inv[s], 0.0) + beta + beta_t
        quad = jnp.sum(jnp.sum(resid[s] * beta, axis=0, keepdims=True), axis=1, keepdims=True)
        left_n = jnp.concatenate([x1, x2, x3], axis=0) * jnp.where(lane1 < BS, -1.0, 1.0)
        left_o = jnp.where(real, eye, 0.0)
        prod = mul2(jnp.concatenate([left_n, left_o], axis=0), mid)
        trace = jnp.sum(
            jnp.sum(prod[: 3 * B] * left_n, axis=0, keepdims=True)
            + jnp.sum(prod[3 * B :] * left_o, axis=0, keepdims=True),
            axis=1,
            keepdims=True,
        )
        t2 = 0.5 * nug * trace
        t1_ = 0.5 * quad - 0.5 * BS - t2
        ph, plo = split2(prod)
        lh, llo = split2(left_n)
        g_n = dot(
            jnp.concatenate([ph, plo], axis=1), jnp.concatenate([lh, lh], axis=1), NT
        ) + dot(ph, llo, NT)
        for i in range(4):
            rows = slice(i * B, (i + 1) * B)
            k_ref[s, rows, : 3 * B] = g_n[rows] * e_ref[s, rows, : 3 * B]
            k_ref[s, rows, 3 * B :] = jnp.where(lane < BS, prod[rows], 0.0) * e_ref[s, rows, 3 * B :]
        z = z_ref[s]
        rhs = jnp.concatenate([z, jnp.ones_like(z)], axis=1)
        hi, low = split2(k_ref[s])
        pz = dot(hi, rhs) + dot(low, rhs)
        zf = z.astype(F32)
        grad = (3.0 * var * inv_sq) * (pz[:, :B] - pz[:, B:] * zf)
        t0 = -jnp.sum(jnp.sum(grad * zf, axis=0, keepdims=True), axis=1, keepdims=True)
        hyper = hyper + jnp.where(lane1 == 0, t0, 0.0) + jnp.where(lane1 == 1, t1_, 0.0)
        hyper = hyper + jnp.where(lane1 == 2, t2, 0.0)
        for k in range(NMAX + 1):
            w = wins[s][k]
            gw_ref[w] = gw_ref[w] + grad[k * BS : (k + 1) * BS]

        mat = schur[s][:BS]
        logdet = jnp.zeros((1, 1), F32)
        for k in range(BS):
            base = (k // 8) * 8
            row = mat[k - (BS - mat.shape[0]) : k - (BS - mat.shape[0]) + 1]
            pivot = row[:, k : k + 1]
            logdet = logdet + jnp.log(pivot)
            if k < BS - 1:
                if (k + 1) % 8 == 0:
                    col = mat[8:, k : k + 1]
                    mat = mat[8:] - col * (row / pivot)
                else:
                    mat = mat - mat[:, k : k + 1] * (row / pivot)
        ll = (-0.5 * quad - 0.5 * logdet) * (1.0 / BS) - 0.5 * LOG_TWO_PI
        ll_ref[s] = jnp.sum(ll)
    hyp_ref[...] = jnp.broadcast_to(hyper, (8, B))


def reduce_kernel(
    x_ref, ps_ref, w_in_ref, b_ref, w_out_ref, gw_ref, hyp_ref,
    fg_ref, gwin_ref, gwout_ref, small_ref,
    out_buf, in_buf, part, part_in, red, red_in, gath,
    g_send, g_recv, s1, r1, s2, r2, s3, r3,
):
    total = lax.axis_size("region") * lax.axis_size("dev")
    region, dev = lax.axis_index("region"), lax.axis_index("dev")
    me = my_index()
    x, core, y, zz = region // 2, region % 2, dev // 8, dev % 8
    g1 = core * 8 + zz
    g2 = x * 4 + y

    def mate1(k):
        other = lax.rem(g1 + k, 16)
        return other, (x * 2 + other // 8, y * 8 + other % 8)

    def mate2(k):
        other = lax.rem(g2 + k, 16)
        return other, ((other // 4) * 2 + core, (other % 4) * 8 + zz)

    barrier = pltpu.get_barrier_semaphore()
    for k in range(1, WIN + 1):
        pl.semaphore_signal(barrier, inc=1, device_id=device(lax.rem(me + k, total)), device_id_type=MESH)
    for k in range(1, 16):
        pl.semaphore_signal(barrier, inc=1, device_id=mate1(k)[1], device_id_type=MESH)
        pl.semaphore_signal(barrier, inc=1, device_id=mate2(k)[1], device_id_type=MESH)
    for k in range(1, WIN + 1):
        out_buf[k - 1, :BS, :] = gw_ref[2 * k].astype(BF16)
        out_buf[k - 1, BS:, :] = gw_ref[2 * k + 1].astype(BF16)
    pl.semaphore_wait(barrier, WIN + 30)
    copies = []
    for k in range(1, WIN + 1):
        copies.append(
            pltpu.make_async_remote_copy(
                src_ref=out_buf.at[k - 1],
                dst_ref=in_buf.at[k - 1],
                send_sem=g_send.at[k - 1],
                recv_sem=g_recv.at[k - 1],
                device_id=device(lax.rem(me + total - k, total)),
                device_id_type=MESH,
            )
        )
        copies[-1].start()
    xs = x_ref[...]
    pre, sig, hidden = network(xs, w_in_ref[...], b_ref[...], w_out_ref[...])
    perm = one_hot(ps_ref[...], ROWS, 0)
    for c in copies:
        c.wait()
    grad = jnp.concatenate([gw_ref[0], gw_ref[1]], axis=0)
    for k in range(WIN):
        grad = grad + in_buf[k].astype(F32)
    hi, lo = split2(grad)
    both = dot(perm, jnp.concatenate([hi, lo], axis=1), TN)
    fg = both[:, :H] + both[:, H:]
    fg_ref[...] = fg
    hi, lo = split2(fg)
    back = dot(hi, w_out_ref[...], NT) + dot(lo, w_out_ref[...], NT)
    dpre = back * sig * (1.0 + pre * (1.0 - sig))
    w_out_part = dot(hidden, jnp.concatenate([hi, lo], axis=1), TN)
    w_out_part = w_out_part[:, :H] + w_out_part[:, H:]
    dhi, dlo = split2(dpre)
    w_in_part = dot(xs, jnp.concatenate([dhi, dlo], axis=1), TN)
    w_in_part = w_in_part[:, :H] + w_in_part[:, H:]
    row = lax.broadcasted_iota(jnp.int32, (8, H), 0)
    extra = jnp.where(row == 0, jnp.sum(dpre, axis=0, keepdims=True), 0.0)
    extra = jnp.where(row == 1, hyp_ref[...], extra)
    for c in range(16):
        src = w_in_part if c < 8 else w_out_part
        part[c, :16, :] = src[(c % 8) * 16 : (c % 8) * 16 + 16]
        part[c, 16:, :] = extra

    copies = []
    for k in range(1, 16):
        other, place = mate1(k)
        copies.append(
            pltpu.make_async_remote_copy(
                src_ref=part.at[other],
                dst_ref=part_in.at[g1],
                send_sem=s1.at[k],
                recv_sem=r1.at[k],
                device_id=place,
                device_id_type=MESH,
            )
        )
        copies[-1].start()
    part_in[g1] = part[g1]
    for c in copies:
        c.wait()
    acc = part_in[0]
    for c in range(1, 16):
        acc = acc + part_in[c]
    red[...] = acc

    copies = []
    for k in range(1, 16):
        _, place = mate2(k)
        copies.append(
            pltpu.make_async_remote_copy(
                src_ref=red,
                dst_ref=red_in.at[g2],
                send_sem=s2.at[k],
                recv_sem=r2.at[k],
                device_id=place,
                device_id_type=MESH,
            )
        )
        copies[-1].start()
    red_in[g2] = red[...]
    for c in copies:
        c.wait()
    acc = red_in[0]
    for c in range(1, 16):
        acc = acc + red_in[c]
    acc = acc * (1.0 / (total * ROWS))
    small_ref[...] = acc[16:]
    gath[g1] = acc[:16]
    copies = []
    for k in range(1, 16):
        _, place = mate1(k)
        copies.append(
            pltpu.make_async_remote_copy(
                src_ref=gath.at[g1],
                dst_ref=gath.at[g1],
                send_sem=s3.at[k],
                recv_sem=r3.at[k],
                device_id=place,
                device_id_type=MESH,
            )
        )
        copies[-1].start()
    for c in copies:
        c.wait()
    for c in range(8):
        gwin_ref[c * 16 : c * 16 + 16, :] = gath[c]
        gwout_ref[c * 16 : c * 16 + 16, :] = gath[8 + c]


VM = pl.BlockSpec(memory_space=pltpu.VMEM)
SM = pl.BlockSpec(memory_space=pltpu.SMEM)
DMA = pltpu.SemaphoreType.DMA


def shards(
    inputs, responses, point_slot, block_home, nbr_ids, nbr_count, w_in, b_in, w_out, kernel_params
):
    place_row = point_slot.reshape(1, ROWS)
    bias = b_in.reshape(1, H)
    window = pl.pallas_call(
        send_kernel,
        out_shape=jax.ShapeDtypeStruct((WIN + 1, ROWS + 16, H), BF16),
        in_specs=[VM] * 6,
        out_specs=VM,
        scratch_shapes=[DMA((WIN,)), DMA((WIN,))],
        compiler_params=pltpu.CompilerParams(collective_id=0, has_side_effects=True),
        name="send_features",
    )(inputs, responses.reshape(1, ROWS), place_row, w_in, bias, w_out)
    loglik, hyper, grads = pl.pallas_call(
        block_kernel,
        out_shape=(
            jax.ShapeDtypeStruct((BPD,), F32),
            jax.ShapeDtypeStruct((8, B), F32),
            jax.ShapeDtypeStruct(((WIN + 1) * BPD, BS, H), F32),
        ),
        in_specs=[SM] * 4 + [VM],
        out_specs=(SM, VM, VM),
        scratch_shapes=[
            pltpu.VMEM((BPD, N, H), BF16),
            pltpu.VMEM((BPD, N, N), F32),
            pltpu.VMEM((BPD, N, N), F32),
        ],
        compiler_params=pltpu.CompilerParams(vmem_limit_bytes=48 * 1024 * 1024),
        name="block_gradients",
    )(block_home, nbr_ids, nbr_count, kernel_params, window)
    feature_grad, g_in, g_out, small = pl.pallas_call(
        reduce_kernel,
        out_shape=(
            jax.ShapeDtypeStruct((ROWS, H), F32),
            jax.ShapeDtypeStruct((H, H), F32),
            jax.ShapeDtypeStruct((H, H), F32),
            jax.ShapeDtypeStruct((8, H), F32),
        ),
        in_specs=[VM] * 7,
        out_specs=(VM,) * 4,
        scratch_shapes=[
            pltpu.VMEM((WIN, ROWS, H), BF16),
            pltpu.VMEM((WIN, ROWS, H), BF16),
            pltpu.VMEM((16, 24, H), F32),
            pltpu.VMEM((16, 24, H), F32),
            pltpu.VMEM((24, H), F32),
            pltpu.VMEM((16, 24, H), F32),
            pltpu.VMEM((16, 16, H), F32),
            DMA((WIN,)),
            DMA((WIN,)),
        ]
        + [DMA((16,))] * 6,
        compiler_params=pltpu.CompilerParams(collective_id=1, has_side_effects=True),
        name="reduce_gradients",
    )(inputs, place_row, w_in, bias, w_out, grads, hyper)
    return loglik, feature_grad, g_in, small[0], g_out, small[1, :3]


def solution(mesh):
    placed = (
        P(("region", "dev"), None),
        P(("region", "dev")),
        P(("region", "dev")),
        P(),
        P(("region", "dev"), None),
        P(("region", "dev")),
        P(),
        P(),
        P(),
        P(),
    )
    return jax.shard_map(
        shards,
        mesh=mesh,
        in_specs=placed,
        out_specs=(P(("region", "dev")), P(("region", "dev"), None), P(), P(), P(), P()),
        check_vma=False,
    )
```

time: 911 us -> 82.2 us (0.09)
  other arithmetic: 396 us -> 0 us
  waiting for transfers between devices: 236 us -> 0 us
  blocking collectives: 78.6 us -> 0 us
  Pallas kernels: 0 us -> 72.2 us
  matrix products: 58.2 us -> 0 us
  local copies, waits for them, and re-layouts: 65.7 us -> 8.92 us
  starting transfers between devices: 42.7 us -> 0 us
  between operations: 29.3 us -> 0.72 us
    another operation x56 -> x0, other arithmetic: 318 us -> none  [the longest x40 236 us: block_loglik(): factor = jnp.linalg.cholesky(kmat)]
    psum x1 -> x0, waiting for transfers between devices: 235 us -> none  [shards(): lax.psum((part_w_in, part_b_in, part_w_out, hyper_sum), ('region', 'dev'))]
    psum x1 -> x0, blocking collectives: 78.6 us -> none  [shards(): lax.psum((part_w_in, part_b_in, part_w_out, hyper_sum), ('region', 'dev'))]
    pallas_call x0 -> x3, Pallas kernels: none -> 72.2 us  [the longest x1 33.5 us: shards(): pl.pallas_call(reduce_kernel, out_shape=(jax.ShapeDtypeStruct((ROWS, H),...]
    scatter-add x4 -> x0, other arithmetic: 54.2 us -> none  [the longest x2 52.6 us: block_loglik(): diag_tail = jnp.diagonal(factor)[-own_rows:]]
    ppermute x9 -> x0, starting transfers between devices: 42.6 us -> none  [passed_along(): lax.ppermute(value, axis, [(source, source + steps) for source in range(l...]
    another operation x68 -> x0, matrix products: 39.4 us -> none  [the longest x40 26.6 us: block_loglik(): factor = jnp.linalg.cholesky(kmat)]
    another operation x93 -> x0, local copies, waits for them, and re-layouts: 32.2 us -> none  [the longest x32 16.1 us: block_loglik(): lax.linalg.triangular_solve(factor, (resp_joint * valid_rows)[:, None], l...]
  transfers between devices with their start and end apart: 10 -> 0, of which waited for: 3 -> 0; matrix products, arithmetic and copies ran while one was open for 1% -> 0% of each run, Pallas kernels for 0% -> 0%
where the time goes in v1:
time: 82.2 us; the launch traced here: 81.9 us
  Pallas kernels  72.2 us (88%)
  local copies, waits for them, and re-layouts  8.92 us (11%)
    pallas_call x1, Pallas kernels, shards(): pl.pallas_call(reduce_kernel, out_shape=(jax.ShapeDtypeStruct((ROWS, H),...  33.5 us
    pallas_call x1, Pallas kernels, shards(): pl.pallas_call(send_kernel, out_shape=jax.ShapeDtypeStruct((WIN + 1, ROWS...  20.4 us
    pallas_call x1, Pallas kernels, shards(): pl.pallas_call(block_kernel, out_shape=(jax.ShapeDtypeStruct((BPD,), F32)...  18.3 us
    unnamed x23, local copies, waits for them, and re-layouts  5.98 us
    squeeze x2, local copies, waits for them, and re-layouts, shards(): return (loglik, feature_grad, g_in, small[0], g_out, small[1, :3])  2.37 us

profile of v1, /device:TPU:1, one launch (start us, length us, event | category | flops | bytes accessed | tf_op | source)
XLA Modules:
  0.0 81.9 jit_solution(14884932660900843654)
XLA Ops:
  0.6 0.0 copy-start.9
  0.6 0.6 copy-done.9
  1.3 0.6 reshape.21.resp_ref
  1.9 0.0 copy-start.3
  1.9 0.0 copy-start.4
  1.9 0.0 copy-start.5
  1.9 0.0 copy-start.6
  1.9 20.4 %send_features.1.win_ref = bf16[4,208,128]{2,1,0:T(8,128)(2,1)} custom-call(bf16[192,128]{1,0:T(8,128)(2,1)} %x_ref.3, bf16[1,192]{1,0:T(2,128)(2,1)} %reshape.21.resp_ref, s32[1,192]{1,0:T(1,128)} %bitcast.6, bf16[128,128]{1,0:T(8,128)(2,1)} %w_in_ref.3, f32[1,128]{1,0:T(1,128)} %bitcast.8, bf16[128,128]{1,0:T(8,128)(2,1)} %w_out_ref.3), custom_call_target="tpu_custom_call" | custom-call | tf_op jit(solution)/shard_map/send_features/pallas_call | solution.py:451
  22.3 0.0 copy-done.3
  22.3 0.0 copy-done.4
  22.3 0.0 copy-done.5
  22.4 0.0 copy-done.6
  22.4 0.0 copy-start
  22.4 0.9 %copy-done = bf16[4,208,128]{2,1,0:T(8,128)(2,1)S(1)} copy-done((bf16[4,208,128]{2,1,0:T(8,128)(2,1)S(1)}, bf16[4,208,128]{2,1,0:T(8,128)(2,1)}, u32[]{:S(2)}) %copy-start) | copy-done | bytes 213016
  23.3 18.3 %block_gradients.1 = (f32[2]{0:T(128)}, f32[8,128]{1,0:T(8,128)S(1)}, f32[8,96,128]{2,1,0:T(8,128)S(1)}) custom-call(s32[512]{0:T(512)S(1)} %copy-done.3, s32[2,4]{1,0:T(2,128)S(1)} %copy-done.4, s32[2]{0:T(128)S(1)} %copy-done.5, f32[3]{0:T(128)S(1)} %copy-done.6, bf16[4,208,128]{2,1,0:T(8,128)(2,1)S(1)} %copy-done), custom_call_target="tpu_custom_call" | custom-call | tf_op jit(solution)/shard_map/block_gradients/pallas_call | solution.py:460
  41.6 0.0 copy-start.1
  41.6 0.7 copy-done.1
  42.3 0.0 copy-start.2
  42.3 0.6 copy-done.2
  42.9 33.5 %reduce_gradients.1 = (f32[192,128]{1,0:T(8,128)}, f32[128,128]{1,0:T(8,128)}, f32[128,128]{1,0:T(8,128)}, f32[8,128]{1,0:T(8,128)}) custom-call(bf16[192,128]{1,0:T(8,128)(2,1)} %x_ref.3, s32[1,192]{1,0:T(1,128)} %bitcast.7, bf16[128,128]{1,0:T(8,128)(2,1)} %w_in_ref.3, f32[1,128]{1,0:T(1,128)} %bitcast.9, bf16[128,128]{1,0:T(8,128)(2,1)} %w_out_ref.3, ...), custom_call_target="tpu_custom_call" | custom-call | tf_op jit(solution)/shard_map/reduce_gradients/pallas_call | solution.py:477
  76.4 1.2 %slice_bitcast_fusion = f32[3]{0:T(128)} fusion(f32[8,128]{1,0:T(8,128)} %get-tuple-element.18), kind=kLoop, calls=%fused_computation | loop fusion | bytes 24 | tf_op jit(solution)/shard_map/squeeze | solution.py:502
  77.6 1.2 %slice_bitcast_fusion.1 = f32[128]{0:T(128)} fusion(f32[8,128]{1,0:T(8,128)} %get-tuple-element.18), kind=kLoop, calls=%fused_computation.1 | loop fusion | bytes 1024 | tf_op jit(solution)/shard_map/squeeze | solution.py:502
  78.8 0.0 copy-start.8
  78.8 1.6 %copy.19 = f32[192,128]{1,0:T(8,128)} copy(f32[192,128]{1,0:T(8,128)} %get-tuple-element.27) | data formatting | bytes 196608
  80.4 0.0 copy-done.8
  80.4 0.0 copy-start.7
  80.4 0.6 copy.20
  81.0 0.2 copy-done.7
  81.3 0.6 copy.21
Async XLA Ops:
  0.6 0.7 copy-start.9
  1.9 20.5 %copy-start.3 = (s32[512]{0:T(512)S(1)}, s32[512]{0:T(512)}, u32[]{:S(2)}) copy-start(s32[512]{0:T(512)} %home_ref.1) | copy-start | bytes 6148
  1.9 20.5 %copy-start.4 = (s32[2,4]{1,0:T(2,128)S(1)}, s32[2,4]{1,0:T(2,128)}, u32[]{:S(2)}) copy-start(s32[2,4]{1,0:T(2,128)} %ids_ref.1) | copy-start | bytes 100
  1.9 20.5 %copy-start.5 = (s32[2]{0:T(128)S(1)}, s32[2]{0:T(128)}, u32[]{:S(2)}) copy-start(s32[2]{0:T(128)} %cnt_ref.1) | copy-start | bytes 28
  1.9 20.5 %copy-start.6 = (f32[3]{0:T(128)S(1)}, f32[3]{0:T(128)}, u32[]{:S(2)}) copy-start(f32[3]{0:T(128)} %par_ref.1) | copy-start | bytes 40
  22.4 0.9 %copy-start = (bf16[4,208,128]{2,1,0:T(8,128)(2,1)S(1)}, bf16[4,208,128]{2,1,0:T(8,128)(2,1)}, u32[]{:S(2)}) copy-start(bf16[4,208,128]{2,1,0:T(8,128)(2,1)} %send_features.1.win_ref) | copy-start | bytes 638980
  41.6 0.7 copy-start.1
  42.3 0.6 copy-start.2
  78.8 1.6 %copy-start.8 = (f32[128,128]{1,0:T(8,128)S(1)}, f32[128,128]{1,0:T(8,128)}, u32[]{:S(2)}) copy-start(f32[128,128]{1,0:T(8,128)} %get-tuple-element.28) | copy-start | bytes 196612
  80.4 0.9 %copy-start.7 = (f32[128,128]{1,0:T(8,128)S(1)}, f32[128,128]{1,0:T(8,128)}, u32[]{:S(2)}) copy-start(f32[128,128]{1,0:T(8,128)} %get-tuple-element.30) | copy-start | bytes 196612

commit v2 on v0

v2 whole, which is shorter than its diff:
```python
import math

import jax
import jax.numpy as jnp
from jax import lax
from jax.experimental import pallas as pl
from jax.experimental.pallas import tpu as pltpu
from jax.sharding import PartitionSpec as P

H = 128
BS = 96
BPD = 2
NMAX = 4
WIN = 3
ROWS = BPD * BS
B = 128
N = 4 * B
STEPS = 8
GROUP = 16
CHUNK = 16

SQRT_THREE = math.sqrt(3.0)
LOG_TWO_PI = math.log(2.0 * math.pi)
MESH = pl.DeviceIdType.MESH
F32 = jnp.float32
BF16 = jnp.bfloat16


def dot(a, b, contract=((1,), (0,))):
    return lax.dot_general(a, b, (contract, ((), ())), preferred_element_type=F32)


NT = ((1,), (1,))
TN = ((0,), (0,))


def split2(a):
    hi = a.astype(BF16)
    return hi, (a - hi.astype(F32)).astype(BF16)


def split3(a):
    hi = a.astype(BF16)
    rest = a - hi.astype(F32)
    mid = rest.astype(BF16)
    return hi, mid, (rest - mid.astype(F32)).astype(BF16)


def lanes(*parts):
    return jnp.concatenate(parts, axis=1)


def rows_of(*parts):
    return jnp.concatenate(parts, axis=0)


def mul2(a, b):
    n = b.shape[1]
    pair = lanes(*split2(b))
    out = dot(lanes(*split2(a)), rows_of(pair, pair))
    return out[:, :n] + out[:, n:]


def mul3(a, b):
    ah, am, al = a if isinstance(a, tuple) else split3(a)
    bh, bm, bl = b if isinstance(b, tuple) else split3(b)
    n = bh.shape[1]
    pair = lanes(bh, bm)
    out = dot(lanes(ah, am), rows_of(pair, pair))
    low = dot(lanes(ah, al), rows_of(bl, bh))
    return out[:, :n] + (out[:, n:] + low)


def mul3_nt(a, b):
    ah, am, al = a
    bh, bm, bl = b
    n = bh.shape[0]
    pair = rows_of(bh, bm)
    out = dot(lanes(ah, am), lanes(pair, pair), NT)
    low = dot(lanes(ah, al), lanes(bl, bh), NT)
    return out[:, :n] + (out[:, n:] + low)


def eye_of(n):
    return (
        lax.broadcasted_iota(jnp.int32, (n, n), 0) == lax.broadcasted_iota(jnp.int32, (n, n), 1)
    ).astype(F32)


def inverses(mats, eye, coef, scales):
    res = [eye - coef * a for a in mats]
    inv = [(scales[0] * coef) * (eye + r) for r in res]
    res = [(1.0 - scales[0]) * eye + scales[0] * mul3(r, r) for r in res]
    for j in range(1, STEPS):
        s = scales[j]
        if j < STEPS - 1:
            both = [mul3(rows_of(x, r), r) for x, r in zip(inv, res)]
            inv = [s * (x + b[:B]) for x, b in zip(inv, both)]
            res = [(1.0 - s) * eye + s * b[B:] for b in both]
        else:
            inv = [s * (x + mul3(x, r)) for x, r in zip(inv, res)]
    return inv


def device(index):
    per = lax.axis_size("dev")
    return (index // per, index % per)


def my_index():
    return lax.axis_index("region") * lax.axis_size("dev") + lax.axis_index("dev")


def network(x, w_in, b_in, w_out):
    pre = dot(x, w_in) + b_in
    sig = 1.0 / (1.0 + jnp.exp(-pre))
    hidden = (pre * sig).astype(BF16)
    return pre, sig, hidden


def one_hot(point_slot, rows, first):
    slot = lax.broadcasted_iota(jnp.int32, (rows, ROWS), 0) + first
    return (slot == point_slot).astype(F32).astype(BF16)


def block(ref, s, a, b):
    return ref[s, a * B : (a + 1) * B, b * B : (b + 1) * B]


def member_windows(me, home_ref, ids_ref, cnt_ref, s):
    places = []
    for k in range(NMAX):
        slot = home_ref[ids_ref[s, k]]
        live = k < cnt_ref[s]
        w = jnp.where(live, (me - slot // BPD) * BPD + slot % BPD, 0)
        places.append((jnp.clip(w, 0, (WIN + 1) * BPD - 1), jnp.where(live, 1.0, 0.0)))
    return places


def kernel_matrix(s, count, places, feat_ref, resp_ref, z_ref, e_ref, k_ref, inv_sq, var, nug, eye):
    lane1 = lax.broadcasted_iota(jnp.int32, (1, B), 1)
    y_row = jnp.zeros((1, N), F32)
    for k, (w, flag) in enumerate(places + [(s, None)]):
        member = feat_ref[w]
        resp = jnp.where(lane1 < BS, resp_ref[w][0:1].astype(F32), 0.0)
        if flag is not None:
            member = (member.astype(F32) * flag).astype(BF16)
            resp = resp * flag
        z_ref[s, k * BS : (k + 1) * BS, :] = member
        resp = lanes(resp, jnp.zeros((1, N - B), F32))
        y_row = y_row + (pltpu.roll(resp, k * BS, 1) if k else resp)
    z_ref[s, (NMAX + 1) * BS :, :] = jnp.zeros((N - (NMAX + 1) * BS, H), BF16)
    z = z_ref[s]
    gram = dot(z, z, NT)
    diag = [jnp.where(eye > 0.0, gram[i * B : (i + 1) * B, i * B : (i + 1) * B], 0.0) for i in range(4)]
    sq_row = lanes(*[jnp.sum(d, axis=0, keepdims=True) for d in diag])
    col_id = lax.broadcasted_iota(jnp.int32, (1, N), 1)
    own = (col_id >= NMAX * BS) & (col_id < (NMAX + 1) * BS)
    v_row = jnp.where((col_id < count * BS) | own, 1.0, 0.0)
    for i in range(4):
        row_id = lax.broadcasted_iota(jnp.int32, (B, 1), 0) + i * B
        own = (row_id >= NMAX * BS) & (row_id < (NMAX + 1) * BS)
        v_col = jnp.where((row_id < count * BS) | own, 1.0, 0.0)
        sq_col = jnp.sum(diag[i], axis=1, keepdims=True)
        mine = slice(i * B, (i + 1) * B)
        for c in range(0, B, 32):
            part = slice(c, c + 32)
            out = slice(i * B + c, i * B + c + 32)
            d2 = jnp.maximum(sq_col[part] + sq_row - 2.0 * gram[out], 0.0)
            r2 = d2 * inv_sq + 1e-06
            rad = SQRT_THREE * (r2 * lax.rsqrt(r2))
            e = jnp.exp(-rad) * (v_col[part] * v_row)
            e_ref[s, out, :] = e
            wide = (i + 1) * B
            kern = var * (1.0 + rad[:, :wide]) * e[:, :wide]
            spot = kern[:, i * B :] + eye[part] * (nug * v_col[part] + 1.0 - v_col[part])
            k_ref[s, out, :wide] = lanes(kern[:, : i * B], spot) if i else spot
    k_ref[s, 3 * B + BS : 3 * B + BS + 1, :] = y_row


def eliminate(both, k_ref, eye, coef, scales):
    invs = []
    for i in range(3):
        lo = (i + 1) * B
        cols = slice(i * B, lo)
        cur = inverses([block(k_ref, s, i, i) for s in both], eye, coef, scales)
        invs.append([split3(c) for c in cur])
        below = [split3(k_ref[s, lo:, cols]) for s in both]
        panel = [split3(mul3(below[s], invs[i][s])) for s in both]
        for b in range(i + 1, 4):
            first = (b - i - 1) * B
            for s in both:
                at = slice(b * B, (b + 1) * B)
                k_ref[s, b * B :, at] = k_ref[s, b * B :, at] - mul3_nt(
                    tuple(p[first:] for p in panel[s]), tuple(p[first : first + B] for p in below[s])
                )
    return invs


def joint_gradient(s, invs, s_inv, resid, z_ref, e_ref, k_ref, var, inv_sq, nug, eye, real):
    sub = lax.broadcasted_iota(jnp.int32, (B, B), 0)
    lane = lax.broadcasted_iota(jnp.int32, (B, B), 1)
    x3 = mul3(block(k_ref, s, 3, 2), invs[2][s])
    p3 = split3(x3)
    x2 = mul3(block(k_ref, s, 3, 1) - mul3(p3, block(k_ref, s, 2, 1)), invs[1][s])
    p2 = split3(x2)
    t1 = block(k_ref, s, 3, 0) - mul3(p3, block(k_ref, s, 2, 0)) - mul3(p2, block(k_ref, s, 1, 0))
    x1 = mul3(t1, invs[0][s])
    sign = jnp.where(lax.broadcasted_iota(jnp.int32, (B, 1), 0) < BS, -1.0, 1.0)
    ys = [x1 * sign, x2 * sign, x3 * sign]
    own = jnp.where(real, eye, 0.0)
    beta_m = mul3(resid, s_inv)
    beta_row = beta_m[BS : BS + 1]
    beta_col = jnp.sum(eye * beta_row, axis=1, keepdims=True)
    mid = jnp.where(real, beta_col * beta_row - s_inv, 0.0) + beta_m
    mid = mid + jnp.where((lane == BS) & (sub < BS), beta_col, 0.0)
    quad = jnp.sum(jnp.sum(resid * beta_m, axis=0, keepdims=True), axis=1, keepdims=True)
    y = lanes(*ys, own)
    prod = mul2(mid, y)
    trace = jnp.sum(jnp.sum(prod * y, axis=0, keepdims=True), axis=1, keepdims=True)
    t2 = 0.5 * nug * trace
    t1 = 0.5 * quad - 0.5 * BS - t2
    w = rows_of(*[m.T for m in ys])
    g = mul2(w, prod)
    low = jnp.where(lax.broadcasted_iota(jnp.int32, (B, 1), 0) < BS, prod, 0.0)
    weights = rows_of(
        (g * e_ref[s, : 3 * B, :]).astype(BF16), (low * e_ref[s, 3 * B :, :]).astype(BF16)
    )
    z = z_ref[s]
    pz = dot(weights, lanes(z, jnp.ones_like(z)))
    zf = z.astype(F32)
    grad = (3.0 * var * inv_sq) * (pz[:, :H] - pz[:, H:] * zf)
    t0 = -jnp.sum(jnp.sum(grad * zf, axis=0, keepdims=True), axis=1, keepdims=True)
    lane1 = lax.broadcasted_iota(jnp.int32, (1, B), 1)
    hyper = jnp.where(lane1 == 0, t0, 0.0) + jnp.where(lane1 == 1, t1, 0.0)
    return grad, hyper + jnp.where(lane1 == 2, t2, 0.0), quad


def log_likelihood(mat, quad):
    mat = mat[:BS]
    pivots = []
    for k in range(BS):
        at = k - (BS - mat.shape[0])
        row = mat[at : at + 1]
        pivots.append(row[:, k : k + 1])
        if k < BS - 1:
            if (k + 1) % 8 == 0:
                mat = mat[8:]
                mat = mat - mat[:, k : k + 1] * (row / pivots[-1])
            else:
                mat = mat - mat[:, k : k + 1] * (row / pivots[-1])
    logdet = jnp.zeros((1, 1), F32)
    for p in pivots:
        logdet = logdet + jnp.log(p)
    return (-0.5 * quad - 0.5 * logdet) * (1.0 / BS) - 0.5 * LOG_TWO_PI


def main_kernel(
    x_ref, resp_ref, ps_ref, w_in_ref, b_ref, w_out_ref, home_ref, ids_ref, cnt_ref, par_ref,
    ll_ref, fg_ref, gath, ext_ref,
    win_ref, wresp_ref, feat_ref, hid_ref, dsil_ref, z_ref, e_ref, k_ref, gw_ref,
    out_buf, in_buf, part, part_in, red, red_in,
    f_send, f_recv, y_send, y_recv, g_send, g_recv, s1, r1, s2, r2, s3, r3,
):
    total = lax.axis_size("region") * lax.axis_size("dev")
    region, dev = lax.axis_index("region"), lax.axis_index("dev")
    me = my_index()
    x, core, y, z = region // 2, region % 2, dev // 8, dev % 8
    ga = x * 4 + y
    gb = core * 8 + z

    def mate_a(k):
        other = lax.rem(ga + k, GROUP)
        return other, ((other // 4) * 2 + core, (other % 4) * 8 + z)

    def mate_b(k):
        other = lax.rem(gb + k, GROUP)
        return other, (x * 2 + other // 8, y * 8 + other % 8)

    def send(src, dst, ssem, rsem, place):
        copy = pltpu.make_async_remote_copy(
            src_ref=src, dst_ref=dst, send_sem=ssem, recv_sem=rsem, device_id=place, device_id_type=MESH
        )
        copy.start()
        return copy

    def later(k):
        return device(lax.rem(me + k + total, total))

    barrier = pltpu.get_barrier_semaphore()
    for k in range(1, WIN + 1):
        pl.semaphore_signal(barrier, inc=1, device_id=later(k), device_id_type=MESH)
        pl.semaphore_signal(barrier, inc=1, device_id=later(-k), device_id_type=MESH)
    for k in range(1, GROUP):
        pl.semaphore_signal(barrier, inc=1, device_id=mate_a(k)[1], device_id_type=MESH)
        pl.semaphore_signal(barrier, inc=1, device_id=mate_b(k)[1], device_id_type=MESH)

    point_slot = ps_ref[...]
    win_ref[0] = dot(one_hot(point_slot, ROWS, 0), x_ref[...]).astype(BF16)
    resp = jnp.broadcast_to(resp_ref[...].astype(F32), (16, ROWS)).astype(BF16)
    wresp_ref[0] = dot(resp, one_hot(point_slot, B, 0), NT).astype(BF16)
    wresp_ref[1] = dot(resp, one_hot(point_slot, B, BS), NT).astype(BF16)
    pl.semaphore_wait(barrier, 2 * WIN + 2 * (GROUP - 1))
    copies = []
    for k in range(1, WIN + 1):
        copies.append(send(win_ref.at[0], win_ref.at[k], f_send.at[k], f_recv.at[k], later(k)))
        copies.append(
            send(
                wresp_ref.at[pl.ds(0, 2)], wresp_ref.at[pl.ds(2 * k, 2)], y_send.at[k], y_recv.at[k], later(k)
            )
        )

    def forward(d):
        pre, sig, hidden = network(win_ref[d], w_in_ref[...], b_ref[...], w_out_ref[...])
        hid_ref[d] = hidden
        dsil_ref[d] = sig * (1.0 + pre * (1.0 - sig))
        feats = dot(hidden, w_out_ref[...]).astype(BF16)
        feat_ref[2 * d] = feats[:BS]
        feat_ref[2 * d + 1] = feats[BS:]

    forward(0)

    def const(v):
        return jnp.full((1, 1), v, F32)

    inv_sq = jnp.exp(-2.0 * const(par_ref[0]))
    var = jnp.exp(const(par_ref[1]))
    nug = jnp.exp(const(par_ref[2]))
    eye = eye_of(B)
    lane = lax.broadcasted_iota(jnp.int32, (B, B), 1)
    sub = lax.broadcasted_iota(jnp.int32, (B, B), 0)
    top = B * var + 1.0
    coef = 2.0 / (top + nug)
    delta = (top - nug) / (top + nug)
    scales = []
    for _ in range(STEPS):
        sq = delta * delta
        scales.append(2.0 / (2.0 - sq))
        delta = sq / (2.0 - sq)
    both = range(BPD)
    places = [member_windows(me, home_ref, ids_ref, cnt_ref, s) for s in both]
    for c in copies:
        c.wait()
    for d in range(1, WIN + 1):
        forward(d)

    for s in both:
        kernel_matrix(
            s, cnt_ref[s], places[s], feat_ref, wresp_ref, z_ref, e_ref, k_ref, inv_sq, var, nug, eye
        )
    invs = eliminate(both, k_ref, eye, coef, scales)
    real = (lane < BS) & (sub < BS)
    last = [block(k_ref, s, 3, 3) for s in both]
    resid = [jnp.where((sub == BS) & (lane < BS), m, 0.0) for m in last]
    schur = [jnp.where(real, m, eye) for m in last]
    s_inv = inverses(schur, eye, coef, scales)
    grads, hypers, quads = [], [], []
    for s in both:
        grad, hyper, quad = joint_gradient(
            s, invs, s_inv[s], resid[s], z_ref, e_ref, k_ref, var, inv_sq, nug, eye, real
        )
        grads.append(grad)
        hypers.append(hyper)
        quads.append(quad)
    for w in range((WIN + 1) * BPD):
        acc = grads[w][NMAX * BS : (NMAX + 1) * BS] if w < BPD else jnp.zeros((BS, H), F32)
        for s in both:
            if w == 1 or (w == 0 and s == 0):
                continue
            for k in range(NMAX):
                place, flag = places[s][k]
                acc = acc + jnp.where(place == w, flag, 0.0) * grads[s][k * BS : (k + 1) * BS]
        gw_ref[w] = acc
        if w >= BPD:
            out_buf[w // BPD - 1, (w % BPD) * BS : (w % BPD + 1) * BS, :] = acc.astype(BF16)
    returns = [
        send(out_buf.at[k - 1], in_buf.at[k - 1], g_send.at[k], g_recv.at[k], later(-k))
        for k in range(1, WIN + 1)
    ]

    w_in_part = jnp.zeros((H, 2 * H), F32)
    w_out_part = jnp.zeros((H, 2 * H), F32)
    b_part = jnp.zeros((1, H), F32)
    for d in range(WIN + 1):
        hi, lo = split2(rows_of(gw_ref[2 * d], gw_ref[2 * d + 1]))
        back = dot(hi, w_out_ref[...], NT) + dot(lo, w_out_ref[...], NT)
        dpre = back * dsil_ref[d]
        w_out_part = w_out_part + dot(hid_ref[d], lanes(hi, lo), TN)
        w_in_part = w_in_part + dot(win_ref[d], lanes(*split2(dpre)), TN)
        b_part = b_part + jnp.sum(dpre, axis=0, keepdims=True)
    w_in_part = (w_in_part[:, :H] + w_in_part[:, H:]).astype(BF16)
    w_out_part = (w_out_part[:, :H] + w_out_part[:, H:]).astype(BF16)
    row = lax.broadcasted_iota(jnp.int32, (16, H), 0)

    def pack(bias, hyper):
        tile = jnp.zeros((16, H), F32)
        for i, part_row in enumerate(split2(bias) + split2(hyper)):
            tile = tile + jnp.where(row == i, part_row.astype(F32), 0.0)
        return tile.astype(BF16)

    def unpack(tile):
        return tile[0:1] + tile[1:2], tile[2:3] + tile[3:4]

    small = pack(b_part, hypers[0] + hypers[1])
    for c in range(GROUP):
        src = w_in_part if c < 8 else w_out_part
        part[c, :CHUNK, :] = src[(c % 8) * CHUNK : (c % 8 + 1) * CHUNK]
        part[c, CHUNK:, :] = small
    copies = []
    for k in range(1, GROUP):
        other, place = mate_a(k)
        copies.append(send(part.at[other], part_in.at[ga], s1.at[k], r1.at[k], place))
    part_in[ga] = part[ga]
    ll_ref[0] = jnp.sum(log_likelihood(schur[0], quads[0]))
    for c in copies:
        c.wait()
    acc = part_in[0].astype(F32)
    for c in range(1, GROUP):
        acc = acc + part_in[c].astype(F32)
    red[:CHUNK, :] = acc[:CHUNK].astype(BF16)
    red[CHUNK:, :] = pack(*unpack(acc[CHUNK:]))

    copies = []
    for k in range(1, GROUP):
        copies.append(send(red, red_in.at[gb], s2.at[k], r2.at[k], mate_b(k)[1]))
    red_in[gb] = red[...]
    ll_ref[1] = jnp.sum(log_likelihood(schur[1], quads[1]))
    for c in copies:
        c.wait()
    acc = red_in[0].astype(F32)
    for c in range(1, GROUP):
        acc = acc + red_in[c].astype(F32)
    gath[ga] = acc[:CHUNK].astype(BF16)
    copies = []
    for k in range(1, GROUP):
        copies.append(send(gath.at[ga], gath.at[ga], s3.at[k], r3.at[k], mate_a(k)[1]))
    bias, hyper = unpack(acc[CHUNK:])
    row8 = lax.broadcasted_iota(jnp.int32, (8, H), 0)
    ext_ref[...] = jnp.where(row8 == 0, bias, 0.0) + jnp.where(row8 == 1, hyper, 0.0)
    for c in returns:
        c.wait()
    grad = rows_of(gw_ref[0], gw_ref[1])
    for k in range(WIN):
        grad = grad + in_buf[k].astype(F32)
    fg_ref[...] = grad
    for c in copies:
        c.wait()


def finish_kernel(ps_ref, ll_in, grad_ref, gath_ref, ext_ref, ll_ref, fg_ref, gin_ref, b_ref, gout_ref, hyp_ref):
    scale = 1.0 / (lax.axis_size("region") * lax.axis_size("dev") * ROWS)
    hi, lo = split2(grad_ref[...])
    both = dot(one_hot(ps_ref[...], ROWS, 0), lanes(hi, lo), TN)
    fg_ref[...] = both[:, :H] + both[:, H:]
    for c in range(8):
        gin_ref[c * CHUNK : (c + 1) * CHUNK, :] = gath_ref[c].astype(F32) * scale
        gout_ref[c * CHUNK : (c + 1) * CHUNK, :] = gath_ref[8 + c].astype(F32) * scale
    ext = ext_ref[...] * scale
    b_ref[...] = ext[0:1].reshape(H)
    for i in range(3):
        hyp_ref[i] = jnp.sum(ext[1:2, i : i + 1])
    for s in range(BPD):
        ll_ref[s] = ll_in[s]


VM = pl.BlockSpec(memory_space=pltpu.VMEM)
SM = pl.BlockSpec(memory_space=pltpu.SMEM)
DMA = pltpu.SemaphoreType.DMA


def shards(
    inputs, responses, point_slot, block_home, nbr_ids, nbr_count, w_in, b_in, w_out, kernel_params
):
    place_row = point_slot.reshape(1, ROWS)
    loglik, grad, gath, ext = pl.pallas_call(
        main_kernel,
        out_shape=(
            jax.ShapeDtypeStruct((BPD,), F32),
            jax.ShapeDtypeStruct((ROWS, H), F32),
            jax.ShapeDtypeStruct((GROUP, CHUNK, H), BF16),
            jax.ShapeDtypeStruct((8, H), F32),
        ),
        in_specs=[VM] * 6 + [SM] * 4,
        out_specs=(SM, VM, VM, VM),
        scratch_shapes=[
            pltpu.VMEM((WIN + 1, ROWS, H), BF16),
            pltpu.VMEM(((WIN + 1) * BPD, 16, H), BF16),
            pltpu.VMEM(((WIN + 1) * BPD, BS, H), BF16),
            pltpu.VMEM((WIN + 1, ROWS, H), BF16),
            pltpu.VMEM((WIN + 1, ROWS, H), F32),
            pltpu.VMEM((BPD, N, H), BF16),
            pltpu.VMEM((BPD, N, N), F32),
            pltpu.VMEM((BPD, N, N), F32),
            pltpu.VMEM(((WIN + 1) * BPD, BS, H), F32),
            pltpu.VMEM((WIN, ROWS, H), BF16),
            pltpu.VMEM((WIN, ROWS, H), BF16),
            pltpu.VMEM((GROUP, 2 * CHUNK, H), BF16),
            pltpu.VMEM((GROUP, 2 * CHUNK, H), BF16),
            pltpu.VMEM((2 * CHUNK, H), BF16),
            pltpu.VMEM((GROUP, 2 * CHUNK, H), BF16),
        ]
        + [DMA((WIN + 1,))] * 6
        + [DMA((GROUP,))] * 6,
        compiler_params=pltpu.CompilerParams(
            collective_id=0, has_side_effects=True, vmem_limit_bytes=48 * 1024 * 1024
        ),
        name="vecchia_main",
    )(
        inputs, responses.reshape(1, ROWS), place_row, w_in, b_in.reshape(1, H), w_out,
        block_home, nbr_ids, nbr_count, kernel_params,
    )
    loglik, feature_grad, g_in, g_b, g_out, hyper = pl.pallas_call(
        finish_kernel,
        out_shape=(
            jax.ShapeDtypeStruct((BPD,), F32),
            jax.ShapeDtypeStruct((ROWS, H), F32),
            jax.ShapeDtypeStruct((H, H), F32),
            jax.ShapeDtypeStruct((H,), F32),
            jax.ShapeDtypeStruct((H, H), F32),
            jax.ShapeDtypeStruct((3,), F32),
        ),
        in_specs=[VM, SM, VM, VM, VM],
        out_specs=(SM, VM, VM, VM, VM, SM),
        name="vecchia_finish",
    )(place_row, loglik, grad, gath, ext)
    return loglik, feature_grad, g_in, g_b, g_out, hyper


def solution(mesh):
    placed = (
        P(("region", "dev"), None),
        P(("region", "dev")),
        P(("region", "dev")),
        P(),
        P(("region", "dev"), None),
        P(("region", "dev")),
        P(),
        P(),
        P(),
        P(),
    )
    return jax.shard_map(
        shards,
        mesh=mesh,
        in_specs=placed,
        out_specs=(P(("region", "dev")), P(("region", "dev"), None), P(), P(), P(), P()),
        check_vma=False,
    )
```

time: 911 us -> 70.6 us (0.08)
  other arithmetic: 396 us -> 0 us
  waiting for transfers between devices: 236 us -> 0 us
  blocking collectives: 78.6 us -> 0 us
  Pallas kernels: 0 us -> 64 us
  local copies, waits for them, and re-layouts: 65.7 us -> 5.37 us
  matrix products: 58.2 us -> 0 us
  starting transfers between devices: 42.7 us -> 0 us
  between operations: 29.3 us -> 0.9 us
    another operation x56 -> x0, other arithmetic: 318 us -> none  [the longest x40 236 us: block_loglik(): factor = jnp.linalg.cholesky(kmat)]
    psum x1 -> x0, waiting for transfers between devices: 235 us -> none  [shards(): lax.psum((part_w_in, part_b_in, part_w_out, hyper_sum), ('region', 'dev'))]
    psum x1 -> x0, blocking collectives: 78.6 us -> none  [shards(): lax.psum((part_w_in, part_b_in, part_w_out, hyper_sum), ('region', 'dev'))]
    pallas_call x0 -> x2, Pallas kernels: none -> 64 us  [the longest x1 62.3 us: shards(): pl.pallas_call(main_kernel, out_shape=(jax.ShapeDtypeStruct((BPD,), F32),...]
    scatter-add x4 -> x0, other arithmetic: 54.2 us -> none  [the longest x2 52.6 us: block_loglik(): diag_tail = jnp.diagonal(factor)[-own_rows:]]
    ppermute x9 -> x0, starting transfers between devices: 42.6 us -> none  [passed_along(): lax.ppermute(value, axis, [(source, source + steps) for source in range(l...]
    another operation x68 -> x0, matrix products: 39.4 us -> none  [the longest x40 26.6 us: block_loglik(): factor = jnp.linalg.cholesky(kmat)]
    another operation x93 -> x0, local copies, waits for them, and re-layouts: 32.2 us -> none  [the longest x32 16.1 us: block_loglik(): lax.linalg.triangular_solve(factor, (resp_joint * valid_rows)[:, None], l...]
  transfers between devices with their start and end apart: 10 -> 0, of which waited for: 3 -> 0; matrix products, arithmetic and copies ran while one was open for 1% -> 0% of each run, Pallas kernels for 0% -> 0%
where the time goes in v2:
time: 70.6 us; the launch traced here: 70.3 us
  Pallas kernels  64 us (91%)
  local copies, waits for them, and re-layouts  5.37 us (8%)
  between operations  0.9 us (1%)
    pallas_call x1, Pallas kernels, shards(): pl.pallas_call(main_kernel, out_shape=(jax.ShapeDtypeStruct((BPD,), F32),...  62.3 us
    unnamed x26, local copies, waits for them, and re-layouts  4.68 us
    pallas_call x1, Pallas kernels, shards(): pl.pallas_call(finish_kernel, out_shape=(jax.ShapeDtypeStruct((BPD,), F32...  1.79 us

profile of v2, /device:TPU:1, one launch (start us, length us, event | category | flops | bytes accessed | tf_op | source)
XLA Modules:
  0.0 70.3 jit_solution(4689925899002753295)
XLA Ops:
  0.6 0.0 copy-start.8
  0.6 0.0 copy-start.10
  0.7 0.0 copy-start.11
  0.7 0.0 copy-start.7
  0.7 0.0 copy-start.5
  0.7 0.0 copy-start.9
  0.7 0.7 reshape.22.resp_ref
  1.4 0.0 copy-done.8
  1.4 0.0 copy-done.10
  1.4 0.0 copy-done.11
  1.4 0.0 copy-done.7
  1.4 0.0 copy-done.5
  1.4 0.0 copy-done.9
  1.4 0.0 copy-start.2
  1.4 0.8 %copy-done.2 = bf16[192,128]{1,0:T(8,128)(2,1)S(1)} copy-done((bf16[192,128]{1,0:T(8,128)(2,1)S(1)}, bf16[192,128]{1,0:T(8,128)(2,1)}, u32[]{:S(2)}) %copy-start.2) | copy-done | bytes 49176
  2.2 0.0 copy-start.3
  2.2 0.8 %copy-done.3 = bf16[128,128]{1,0:T(8,128)(2,1)S(1)} copy-done((bf16[128,128]{1,0:T(8,128)(2,1)S(1)}, bf16[128,128]{1,0:T(8,128)(2,1)}, u32[]{:S(2)}) %copy-start.3) | copy-done | bytes 32792
  3.0 0.0 copy-start.4
  3.0 0.8 %copy-done.4 = bf16[128,128]{1,0:T(8,128)(2,1)S(1)} copy-done((bf16[128,128]{1,0:T(8,128)(2,1)S(1)}, bf16[128,128]{1,0:T(8,128)(2,1)}, u32[]{:S(2)}) %copy-start.4) | copy-done | bytes 32792
  3.7 62.3 %vecchia_main.1 = (f32[2]{0:T(128)S(1)}, f32[192,128]{1,0:T(8,128)S(1)}, bf16[16,16,128]{2,1,0:T(8,128)(2,1)S(1)}, f32[8,128]{1,0:T(8,128)S(1)}) custom-call(bf16[192,128]{1,0:T(8,128)(2,1)S(1)} %copy-done.2, bf16[1,192]{1,0:T(2,128)(2,1)S(1)} %reshape.22.resp_ref, s32[1,192]{1,0:T(1,128)S(1)} %bitcast.3, bf16[128,128]{1,0:T(8,128)(2,1)S(1)} %copy-done.3, ...), custom_call_target="tpu_custom_call" | custom-call | tf_op jit(solution)/shard_map/vecchia_main/pallas_call | solution.py:475
  66.0 0.0 copy-start
  66.0 0.6 copy-done
  66.6 0.0 copy-start.1
  66.6 0.6 copy-done.1
  67.3 0.0 copy-start.6
  67.3 0.6 copy-done.6
  67.8 0.0 copy-start.12
  67.8 0.5 copy-done.12
  68.4 1.8 %vecchia_finish.1 = (f32[2]{0:T(128)}, f32[192,128]{1,0:T(8,128)}, f32[128,128]{1,0:T(8,128)}, f32[128]{0:T(128)}, f32[128,128]{1,0:T(8,128)}, /*index=5*/f32[3]{0:T(128)}) custom-call(s32[1,192]{1,0:T(1,128)} %bitcast.2, f32[2]{0:T(128)} %copy-done.12, f32[192,128]{1,0:T(8,128)} %copy-done, bf16[16,16,128]{2,1,0:T(8,128)(2,1)} %copy-done.1, f32[8,128]{1,0:T(8,128)} %copy-done.6), custom_call_target="tpu_custom_call" | custom-call | tf_op jit(solution)/shard_map/vecchia_finish/pallas_call | solution.py:512
Async XLA Ops:
  0.6 0.8 %copy-start.8 = (s32[2,4]{1,0:T(2,128)S(1)}, s32[2,4]{1,0:T(2,128)}, u32[]{:S(2)}) copy-start(s32[2,4]{1,0:T(2,128)} %ids_ref.1) | copy-start | bytes 100
  0.6 0.7 %copy-start.10 = (s32[2]{0:T(128)S(1)}, s32[2]{0:T(128)}, u32[]{:S(2)}) copy-start(s32[2]{0:T(128)} %cnt_ref.1) | copy-start | bytes 28
  0.7 0.7 %copy-start.11 = (f32[3]{0:T(128)S(1)}, f32[3]{0:T(128)}, u32[]{:S(2)}) copy-start(f32[3]{0:T(128)} %par_ref.1) | copy-start | bytes 40
  0.7 0.7 %copy-start.7 = (s32[512]{0:T(512)S(1)}, s32[512]{0:T(512)}, u32[]{:S(2)}) copy-start(s32[512]{0:T(512)} %home_ref.1) | copy-start | bytes 6148
  0.7 0.7 %copy-start.5 = (s32[192]{0:T(256)S(1)}, s32[192]{0:T(256)}, u32[]{:S(2)}) copy-start(s32[192]{0:T(256)} %param.12) | copy-start | bytes 2308
  0.7 0.7 %copy-start.9 = (f32[128]{0:T(128)S(1)}, f32[128]{0:T(128)}, u32[]{:S(2)}) copy-start(f32[128]{0:T(128)} %param.17) | copy-start | bytes 1540
  1.4 0.8 %copy-start.2 = (bf16[192,128]{1,0:T(8,128)(2,1)S(1)}, bf16[192,128]{1,0:T(8,128)(2,1)}, u32[]{:S(2)}) copy-start(bf16[192,128]{1,0:T(8,128)(2,1)} %x_ref.1) | copy-start | bytes 147460
  2.2 0.8 %copy-start.3 = (bf16[128,128]{1,0:T(8,128)(2,1)S(1)}, bf16[128,128]{1,0:T(8,128)(2,1)}, u32[]{:S(2)}) copy-start(bf16[128,128]{1,0:T(8,128)(2,1)} %w_in_ref.1) | copy-start | bytes 98308
  3.0 0.8 %copy-start.4 = (bf16[128,128]{1,0:T(8,128)(2,1)S(1)}, bf16[128,128]{1,0:T(8,128)(2,1)}, u32[]{:S(2)}) copy-start(bf16[128,128]{1,0:T(8,128)(2,1)} %w_out_ref.1) | copy-start | bytes 98308
  66.0 0.6 copy-start
  66.6 0.6 copy-start.1
  67.3 0.6 copy-start.6
  67.8 0.5 copy-start.12

commit v3 on v2

--- a/solution.py
+++ b/solution.py
@@ -18,6 +18,7 @@
 STEPS = 8
 GROUP = 16
 CHUNK = 16
+DEPTH = 8
 
 SQRT_THREE = math.sqrt(3.0)
 LOG_TWO_PI = math.log(2.0 * math.pi)
@@ -236,46 +237,41 @@
     return grad, hyper + jnp.where(lane1 == 2, t2, 0.0), quad
 
 
-def log_likelihood(mat, quad):
-    mat = mat[:BS]
-    pivots = []
-    for k in range(BS):
-        at = k - (BS - mat.shape[0])
-        row = mat[at : at + 1]
-        pivots.append(row[:, k : k + 1])
-        if k < BS - 1:
-            if (k + 1) % 8 == 0:
-                mat = mat[8:]
-                mat = mat - mat[:, k : k + 1] * (row / pivots[-1])
-            else:
-                mat = mat - mat[:, k : k + 1] * (row / pivots[-1])
-    logdet = jnp.zeros((1, 1), F32)
-    for p in pivots:
-        logdet = logdet + jnp.log(p)
-    return (-0.5 * quad - 0.5 * logdet) * (1.0 / BS) - 0.5 * LOG_TWO_PI
+def pivot_steps(mat_ref, log_ref, first, last):
+    mats = [mat_ref[i, first:BS, :] for i in range(BPD)]
+    logdets = [log_ref[i, 0:1, 0:1] for i in range(BPD)]
+    for k in range(first, last):
+        for i, mat in enumerate(mats):
+            at = k - (BS - mat.shape[0])
+            row = mat[at : at + 1]
+            pivot = row[:, k : k + 1]
+            logdets[i] = logdets[i] + jnp.log(pivot)
+            if k < BS - 1:
+                if (k + 1) % 8 == 0:
+                    mat = mat[8:]
+                mats[i] = mat - mat[:, k : k + 1] * (row / pivot)
+    for i in range(BPD):
+        log_ref[i, 0:1, :] = jnp.broadcast_to(logdets[i], (1, B))
+        if last < BS:
+            mat_ref[i, last:BS, :] = mats[i]
 
 
 def main_kernel(
     x_ref, resp_ref, ps_ref, w_in_ref, b_ref, w_out_ref, home_ref, ids_ref, cnt_ref, par_ref,
     ll_ref, fg_ref, gath, ext_ref,
     win_ref, wresp_ref, feat_ref, hid_ref, dsil_ref, z_ref, e_ref, k_ref, gw_ref,
-    out_buf, in_buf, part, part_in, red, red_in,
-    f_send, f_recv, y_send, y_recv, g_send, g_recv, s1, r1, s2, r2, s3, r3,
+    out_buf, in_buf, part, part_in, pair, red_in, mat_ref, log_ref,
+    f_send, f_recv, y_send, y_recv, g_send, g_recv, s1, r1, s2, r2, s3, r3, c_send, c_recv,
 ):
     total = lax.axis_size("region") * lax.axis_size("dev")
     region, dev = lax.axis_index("region"), lax.axis_index("dev")
     me = my_index()
-    x, core, y, z = region // 2, region % 2, dev // 8, dev % 8
+    x, core, y, z = region // 2, region % 2, dev // DEPTH, dev % DEPTH
     ga = x * 4 + y
-    gb = core * 8 + z
 
     def mate_a(k):
         other = lax.rem(ga + k, GROUP)
-        return other, ((other // 4) * 2 + core, (other % 4) * 8 + z)
-
-    def mate_b(k):
-        other = lax.rem(gb + k, GROUP)
-        return other, (x * 2 + other // 8, y * 8 + other % 8)
+        return other, ((other // 4) * 2 + core, (other % 4) * DEPTH + z)
 
     def send(src, dst, ssem, rsem, place):
         copy = pltpu.make_async_remote_copy(
@@ -293,14 +289,17 @@
         pl.semaphore_signal(barrier, inc=1, device_id=later(-k), device_id_type=MESH)
     for k in range(1, GROUP):
         pl.semaphore_signal(barrier, inc=1, device_id=mate_a(k)[1], device_id_type=MESH)
-        pl.semaphore_signal(barrier, inc=1, device_id=mate_b(k)[1], device_id_type=MESH)
-
-    point_slot = ps_ref[...]
+    for k in range(1, DEPTH):
+        place = (region, y * DEPTH + lax.rem(z + k, DEPTH))
+        pl.semaphore_signal(barrier, inc=1, device_id=place, device_id_type=MESH)
+    pl.semaphore_signal(barrier, inc=1, device_id=(x * 2 + 1 - core, dev), device_id_type=MESH)
+
+    point_slot = ps_ref[...].reshape(1, ROWS)
     win_ref[0] = dot(one_hot(point_slot, ROWS, 0), x_ref[...]).astype(BF16)
-    resp = jnp.broadcast_to(resp_ref[...].astype(F32), (16, ROWS)).astype(BF16)
+    resp = jnp.broadcast_to(resp_ref[...].astype(F32).reshape(1, ROWS), (16, ROWS)).astype(BF16)
     wresp_ref[0] = dot(resp, one_hot(point_slot, B, 0), NT).astype(BF16)
     wresp_ref[1] = dot(resp, one_hot(point_slot, B, BS), NT).astype(BF16)
-    pl.semaphore_wait(barrier, 2 * WIN + 2 * (GROUP - 1))
+    pl.semaphore_wait(barrier, 2 * WIN + GROUP + DEPTH - 1)
     copies = []
     for k in range(1, WIN + 1):
         copies.append(send(win_ref.at[0], win_ref.at[k], f_send.at[k], f_recv.at[k], later(k)))
@@ -311,7 +310,7 @@
         )
 
     def forward(d):
-        pre, sig, hidden = network(win_ref[d], w_in_ref[...], b_ref[...], w_out_ref[...])
+        pre, sig, hidden = network(win_ref[d], w_in_ref[...], b_ref[...].reshape(1, H), w_out_ref[...])
         hid_ref[d] = hidden
         dsil_ref[d] = sig * (1.0 + pre * (1.0 - sig))
         feats = dot(hidden, w_out_ref[...]).astype(BF16)
@@ -354,6 +353,8 @@
     resid = [jnp.where((sub == BS) & (lane < BS), m, 0.0) for m in last]
     schur = [jnp.where(real, m, eye) for m in last]
     s_inv = inverses(schur, eye, coef, scales)
+    for s in both:
+        mat_ref[s] = schur[s][:BS]
     grads, hypers, quads = [], [], []
     for s in both:
         grad, hyper, quad = joint_gradient(
@@ -388,20 +389,12 @@
         w_out_part = w_out_part + dot(hid_ref[d], lanes(hi, lo), TN)
         w_in_part = w_in_part + dot(win_ref[d], lanes(*split2(dpre)), TN)
         b_part = b_part + jnp.sum(dpre, axis=0, keepdims=True)
-    w_in_part = (w_in_part[:, :H] + w_in_part[:, H:]).astype(BF16)
-    w_out_part = (w_out_part[:, :H] + w_out_part[:, H:]).astype(BF16)
-    row = lax.broadcasted_iota(jnp.int32, (16, H), 0)
-
-    def pack(bias, hyper):
-        tile = jnp.zeros((16, H), F32)
-        for i, part_row in enumerate(split2(bias) + split2(hyper)):
-            tile = tile + jnp.where(row == i, part_row.astype(F32), 0.0)
-        return tile.astype(BF16)
-
-    def unpack(tile):
-        return tile[0:1] + tile[1:2], tile[2:3] + tile[3:4]
-
-    small = pack(b_part, hypers[0] + hypers[1])
+    w_in_part = w_in_part[:, :H] + w_in_part[:, H:]
+    w_out_part = w_out_part[:, :H] + w_out_part[:, H:]
+    row8 = lax.broadcasted_iota(jnp.int32, (8, H), 0)
+    for s in both:
+        log_ref[s] = jnp.where(row8 == 1, quads[s], 0.0)
+    small = jnp.where(row8 == 0, b_part, 0.0) + jnp.where(row8 == 1, hypers[0] + hypers[1], 0.0)
     for c in range(GROUP):
         src = w_in_part if c < 8 else w_out_part
         part[c, :CHUNK, :] = src[(c % 8) * CHUNK : (c % 8 + 1) * CHUNK]
@@ -411,47 +404,62 @@
         other, place = mate_a(k)
         copies.append(send(part.at[other], part_in.at[ga], s1.at[k], r1.at[k], place))
     part_in[ga] = part[ga]
-    ll_ref[0] = jnp.sum(log_likelihood(schur[0], quads[0]))
+
+    @pl.when(dev >= 0)
+    def _():
+        pivot_steps(mat_ref, log_ref, 0, 32)
+
     for c in copies:
         c.wait()
-    acc = part_in[0].astype(F32)
+    acc = part_in[0]
     for c in range(1, GROUP):
-        acc = acc + part_in[c].astype(F32)
-    red[:CHUNK, :] = acc[:CHUNK].astype(BF16)
-    red[CHUNK:, :] = pack(*unpack(acc[CHUNK:]))
-
+        acc = acc + part_in[c]
+    pair[core] = acc
+    copy = send(pair.at[core], pair.at[core], c_send, c_recv, (x * 2 + 1 - core, dev))
+    copy.wait()
+    red_in[z] = pair[0] + pair[1]
     copies = []
-    for k in range(1, GROUP):
-        copies.append(send(red, red_in.at[gb], s2.at[k], r2.at[k], mate_b(k)[1]))
-    red_in[gb] = red[...]
-    ll_ref[1] = jnp.sum(log_likelihood(schur[1], quads[1]))
+    for k in range(1, DEPTH):
+        place = (region, y * DEPTH + lax.rem(z + k, DEPTH))
+        copies.append(send(red_in.at[z], red_in.at[z], s2.at[k], r2.at[k], place))
+
+    @pl.when(dev >= 0)
+    def _():
+        pivot_steps(mat_ref, log_ref, 32, 64)
+
     for c in copies:
         c.wait()
-    acc = red_in[0].astype(F32)
-    for c in range(1, GROUP):
-        acc = acc + red_in[c].astype(F32)
+    acc = red_in[0]
+    for c in range(1, DEPTH):
+        acc = acc + red_in[c]
     gath[ga] = acc[:CHUNK].astype(BF16)
+    ext_ref[...] = acc[CHUNK:]
     copies = []
     for k in range(1, GROUP):
         copies.append(send(gath.at[ga], gath.at[ga], s3.at[k], r3.at[k], mate_a(k)[1]))
-    bias, hyper = unpack(acc[CHUNK:])
-    row8 = lax.broadcasted_iota(jnp.int32, (8, H), 0)
-    ext_ref[...] = jnp.where(row8 == 0, bias, 0.0) + jnp.where(row8 == 1, hyper, 0.0)
+
+    @pl.when(dev >= 0)
+    def _():
+        pivot_steps(mat_ref, log_ref, 64, BS)
+        for s in both:
+            ll = -0.5 * (log_ref[s, 0:1, 0:1] + log_ref[s, 1:2, 0:1]) * (1.0 / BS) - 0.5 * LOG_TWO_PI
+            ll_ref[s] = jnp.sum(ll)
+
     for c in returns:
         c.wait()
     grad = rows_of(gw_ref[0], gw_ref[1])
     for k in range(WIN):
         grad = grad + in_buf[k].astype(F32)
-    fg_ref[...] = grad
+    perm = one_hot(ps_ref[...].reshape(1, ROWS), ROWS, 0)
+    pairs = dot(perm, lanes(*split2(grad)), TN)
+    fg_ref[...] = pairs[:, :H] + pairs[:, H:]
     for c in copies:
         c.wait()
 
 
-def finish_kernel(ps_ref, ll_in, grad_ref, gath_ref, ext_ref, ll_ref, fg_ref, gin_ref, b_ref, gout_ref, hyp_ref):
+def finish_kernel(ll_in, grad_ref, gath_ref, ext_ref, ll_ref, fg_ref, gin_ref, b_ref, gout_ref, hyp_ref):
     scale = 1.0 / (lax.axis_size("region") * lax.axis_size("dev") * ROWS)
-    hi, lo = split2(grad_ref[...])
-    both = dot(one_hot(ps_ref[...], ROWS, 0), lanes(hi, lo), TN)
-    fg_ref[...] = both[:, :H] + both[:, H:]
+    fg_ref[...] = grad_ref[...]
     for c in range(8):
         gin_ref[c * CHUNK : (c + 1) * CHUNK, :] = gath_ref[c].astype(F32) * scale
         gout_ref[c * CHUNK : (c + 1) * CHUNK, :] = gath_ref[8 + c].astype(F32) * scale
@@ -471,7 +479,6 @@
 def shards(
     inputs, responses, point_slot, block_home, nbr_ids, nbr_count, w_in, b_in, w_out, kernel_params
 ):
-    place_row = point_slot.reshape(1, ROWS)
     loglik, grad, gath, ext = pl.pallas_call(
         main_kernel,
         out_shape=(
@@ -494,19 +501,22 @@
             pltpu.VMEM(((WIN + 1) * BPD, BS, H), F32),
             pltpu.VMEM((WIN, ROWS, H), BF16),
             pltpu.VMEM((WIN, ROWS, H), BF16),
-            pltpu.VMEM((GROUP, 2 * CHUNK, H), BF16),
-            pltpu.VMEM((GROUP, 2 * CHUNK, H), BF16),
-            pltpu.VMEM((2 * CHUNK, H), BF16),
-            pltpu.VMEM((GROUP, 2 * CHUNK, H), BF16),
+            pltpu.VMEM((GROUP, CHUNK + 8, H), F32),
+            pltpu.VMEM((GROUP, CHUNK + 8, H), F32),
+            pltpu.VMEM((2, CHUNK + 8, H), F32),
+            pltpu.VMEM((DEPTH, CHUNK + 8, H), F32),
+            pltpu.VMEM((BPD, BS, B), F32),
+            pltpu.VMEM((BPD, 8, B), F32),
         ]
         + [DMA((WIN + 1,))] * 6
-        + [DMA((GROUP,))] * 6,
+        + [DMA((GROUP,))] * 6
+        + [DMA, DMA],
         compiler_params=pltpu.CompilerParams(
-            collective_id=0, has_side_effects=True, vmem_limit_bytes=48 * 1024 * 1024
+            collective_id=0, has_side_effects=True, vmem_limit_bytes=60 * 1024 * 1024
         ),
         name="vecchia_main",
     )(
-        inputs, responses.reshape(1, ROWS), place_row, w_in, b_in.reshape(1, H), w_out,
+        inputs, responses, point_slot, w_in, b_in, w_out,
         block_home, nbr_ids, nbr_count, kernel_params,
     )
     loglik, feature_grad, g_in, g_b, g_out, hyper = pl.pallas_call(
@@ -519,10 +529,10 @@
             jax.ShapeDtypeStruct((H, H), F32),
             jax.ShapeDtypeStruct((3,), F32),
         ),
-        in_specs=[VM, SM, VM, VM, VM],
+        in_specs=[SM, VM, VM, VM],
         out_specs=(SM, VM, VM, VM, VM, SM),
         name="vecchia_finish",
-    )(place_row, loglik, grad, gath, ext)
+    )(loglik, grad, gath, ext)
     return loglik, feature_grad, g_in, g_b, g_out, hyper
 
 

time: 70.6 us -> 55.9 us (0.79)
  Pallas kernels: 64 us -> 54.9 us
  local copies, waits for them, and re-layouts: 5.37 us -> 0 us
    pallas_call x1, Pallas kernels: 62.3 us -> 53.2 us  [shards(): pl.pallas_call(main_kernel, out_shape=(jax.ShapeDtypeStruct((BPD,), F32),...]
    unnamed x26 -> x0, local copies, waits for them, and re-layouts: 4.68 us -> none
where the time goes in v3:
time: 55.9 us; the launch traced here: 55.7 us
  Pallas kernels  54.9 us (98%)
  between operations  0.8 us (1%)
    pallas_call x1, Pallas kernels, shards(): pl.pallas_call(main_kernel, out_shape=(jax.ShapeDtypeStruct((BPD,), F32),...  53.2 us
    pallas_call x1, Pallas kernels, shards(): pl.pallas_call(finish_kernel, out_shape=(jax.ShapeDtypeStruct((BPD,), F32...  1.65 us

profile of v3, /device:TPU:1, one launch (start us, length us, event | category | flops | bytes accessed | tf_op | source)
XLA Modules:
  0.0 55.7 jit_solution(13627624417762917693)
XLA Ops:
  0.6 53.2 %vecchia_main.1 = (f32[2]{0:T(128)}, f32[192,128]{1,0:T(8,128)}, bf16[16,16,128]{2,1,0:T(8,128)(2,1)}, f32[8,128]{1,0:T(8,128)}) custom-call(bf16[192,128]{1,0:T(8,128)(2,1)} %x_ref.1, bf16[192]{0:T(256)(128)(2,1)} %resp_ref.1, s32[192]{0:T(256)} %ps_ref.1, bf16[128,128]{1,0:T(8,128)(2,1)} %w_in_ref.1, f32[128]{0:T(128)} %b_ref.1, ...), custom_call_target="tpu_custom_call" | custom-call | tf_op jit(solution)/shard_map/vecchia_main/pallas_call | solution.py:482
  53.9 1.7 %vecchia_finish.1 = (f32[2]{0:T(128)}, f32[192,128]{1,0:T(8,128)}, f32[128,128]{1,0:T(8,128)}, f32[128]{0:T(128)}, f32[128,128]{1,0:T(8,128)}, /*index=5*/f32[3]{0:T(128)}) custom-call(f32[2]{0:T(128)} %get-tuple-element.10.ll_in, f32[192,128]{1,0:T(8,128)} %get-tuple-element.11.grad_ref, bf16[16,16,128]{2,1,0:T(8,128)(2,1)} %get-tuple-element.12.gath_ref, ...), custom_call_target="tpu_custom_call" | custom-call | tf_op jit(solution)/shard_map/vecchia_finish/pallas_call | solution.py:522

commit v4 on v3

--- a/solution.py
+++ b/solution.py
@@ -88,19 +88,24 @@
     ).astype(F32)
 
 
-def inverses(mats, eye, coef, scales):
+def inverses(mats, eye, coef, scales, below=None):
     res = [eye - coef * a for a in mats]
     inv = [(scales[0] * coef) * (eye + r) for r in res]
     res = [(1.0 - scales[0]) * eye + scales[0] * mul3(r, r) for r in res]
-    for j in range(1, STEPS):
+    for j in range(1, STEPS - 1):
         s = scales[j]
-        if j < STEPS - 1:
-            both = [mul3(rows_of(x, r), r) for x, r in zip(inv, res)]
-            inv = [s * (x + b[:B]) for x, b in zip(inv, both)]
-            res = [(1.0 - s) * eye + s * b[B:] for b in both]
-        else:
-            inv = [s * (x + mul3(x, r)) for x, r in zip(inv, res)]
-    return inv
+        both = [mul3(rows_of(r, x), r) for x, r in zip(inv, res)]
+        if below is not None and j == STEPS - 2:
+            panel = [mul3(b, x) for b, x in zip(below, inv)]
+            panel = [s * (p + mul3(p, r)) for p, r in zip(panel, res)]
+        inv = [s * (x + b[B:]) for x, b in zip(inv, both)]
+        res = [(1.0 - s) * eye + s * b[:B] for b in both]
+    s = scales[-1]
+    parts = [split3(r) for r in res]
+    if below is not None:
+        panel = [s * (p + mul3(p, r)) for p, r in zip(panel, parts)]
+    inv = [s * (x + mul3(x, r)) for x, r in zip(inv, parts)]
+    return inv if below is None else (inv, panel)
 
 
 def device(index):
@@ -184,10 +189,10 @@
     for i in range(3):
         lo = (i + 1) * B
         cols = slice(i * B, lo)
-        cur = inverses([block(k_ref, s, i, i) for s in both], eye, coef, scales)
+        below = [split3(k_ref[s, lo:, cols]) for s in both]
+        cur, panel = inverses([block(k_ref, s, i, i) for s in both], eye, coef, scales, below)
         invs.append([split3(c) for c in cur])
-        below = [split3(k_ref[s, lo:, cols]) for s in both]
-        panel = [split3(mul3(below[s], invs[i][s])) for s in both]
+        panel = [split3(p) for p in panel]
         for b in range(i + 1, 4):
             first = (b - i - 1) * B
             for s in both:
@@ -224,11 +229,10 @@
     w = rows_of(*[m.T for m in ys])
     g = mul2(w, prod)
     low = jnp.where(lax.broadcasted_iota(jnp.int32, (B, 1), 0) < BS, prod, 0.0)
-    weights = rows_of(
-        (g * e_ref[s, : 3 * B, :]).astype(BF16), (low * e_ref[s, 3 * B :, :]).astype(BF16)
-    )
+    high, rest = split2(rows_of(g * e_ref[s, : 3 * B, :], low * e_ref[s, 3 * B :, :]))
     z = z_ref[s]
-    pz = dot(weights, lanes(z, jnp.ones_like(z)))
+    rhs = lanes(z, jnp.ones_like(z))
+    pz = dot(high, rhs) + dot(rest, rhs)
     zf = z.astype(F32)
     grad = (3.0 * var * inv_sq) * (pz[:, :H] - pz[:, H:] * zf)
     t0 = -jnp.sum(jnp.sum(grad * zf, axis=0, keepdims=True), axis=1, keepdims=True)
@@ -257,11 +261,13 @@
 
 
 def main_kernel(
-    x_ref, resp_ref, ps_ref, w_in_ref, b_ref, w_out_ref, home_ref, ids_ref, cnt_ref, par_ref,
-    ll_ref, fg_ref, gath, ext_ref,
+    x_in, resp_in, ps_in, w_in_in, b_in, w_out_in, home_ref, ids_ref, cnt_ref, par_ref,
+    ll_ref, fg_out, gath, ext_out,
+    x_ref, resp_ref, ps_ref, w_in_ref, b_ref, w_out_ref,
+    fg_ref, mine_ref, ext_ref, in_sem, out_sem,
     win_ref, wresp_ref, feat_ref, hid_ref, dsil_ref, z_ref, e_ref, k_ref, gw_ref,
     out_buf, in_buf, part, part_in, pair, red_in, mat_ref, log_ref,
-    f_send, f_recv, y_send, y_recv, g_send, g_recv, s1, r1, s2, r2, s3, r3, c_send, c_recv,
+    f_send, f_recv, g_send, g_recv, s1, r1, s2, r2, s3, r3, c_send, c_recv,
 ):
     total = lax.axis_size("region") * lax.axis_size("dev")
     region, dev = lax.axis_index("region"), lax.axis_index("dev")
@@ -283,6 +289,11 @@
     def later(k):
         return device(lax.rem(me + k + total, total))
 
+    ops = (x_in, resp_in, ps_in, w_in_in, b_in, w_out_in)
+    refs = (x_ref, resp_ref, ps_ref, w_in_ref, b_ref, w_out_ref)
+    loads = [pltpu.make_async_copy(a, b, in_sem.at[i]) for i, (a, b) in enumerate(zip(ops, refs))]
+    for c in loads:
+        c.start()
     barrier = pltpu.get_barrier_semaphore()
     for k in range(1, WIN + 1):
         pl.semaphore_signal(barrier, inc=1, device_id=later(k), device_id_type=MESH)
@@ -294,28 +305,32 @@
         pl.semaphore_signal(barrier, inc=1, device_id=place, device_id_type=MESH)
     pl.semaphore_signal(barrier, inc=1, device_id=(x * 2 + 1 - core, dev), device_id_type=MESH)
 
+    for c in loads:
+        c.wait()
     point_slot = ps_ref[...].reshape(1, ROWS)
-    win_ref[0] = dot(one_hot(point_slot, ROWS, 0), x_ref[...]).astype(BF16)
+    win_ref[0, :ROWS, :] = dot(one_hot(point_slot, ROWS, 0), x_ref[...]).astype(BF16)
     resp = jnp.broadcast_to(resp_ref[...].astype(F32).reshape(1, ROWS), (16, ROWS)).astype(BF16)
-    wresp_ref[0] = dot(resp, one_hot(point_slot, B, 0), NT).astype(BF16)
-    wresp_ref[1] = dot(resp, one_hot(point_slot, B, BS), NT).astype(BF16)
+    win_ref[0, ROWS : ROWS + 16, :] = dot(resp, one_hot(point_slot, B, 0), NT).astype(BF16)
+    win_ref[0, ROWS + 16 :, :] = dot(resp, one_hot(point_slot, B, BS), NT).astype(BF16)
     pl.semaphore_wait(barrier, 2 * WIN + GROUP + DEPTH - 1)
-    copies = []
-    for k in range(1, WIN + 1):
-        copies.append(send(win_ref.at[0], win_ref.at[k], f_send.at[k], f_recv.at[k], later(k)))
-        copies.append(
-            send(
-                wresp_ref.at[pl.ds(0, 2)], wresp_ref.at[pl.ds(2 * k, 2)], y_send.at[k], y_recv.at[k], later(k)
-            )
-        )
+
+    def shift(src, dst, cut, sem, k):
+        at = pl.ds(cut.start, cut.stop - cut.start)
+        return send(win_ref.at[src, at], win_ref.at[dst, at], f_send.at[sem], f_recv.at[sem], later(k))
+
+    cuts = [slice(0, 64), slice(64, 128), slice(128, ROWS + 32)]
+    two = [shift(0, 2, cut, q, 2) for q, cut in enumerate(cuts)]
+    one = shift(0, 1, slice(0, ROWS + 32), 3, 1)
 
     def forward(d):
-        pre, sig, hidden = network(win_ref[d], w_in_ref[...], b_ref[...].reshape(1, H), w_out_ref[...])
+        pre, sig, hidden = network(win_ref[d, :ROWS, :], w_in_ref[...], b_ref[...].reshape(1, H), w_out_ref[...])
         hid_ref[d] = hidden
         dsil_ref[d] = sig * (1.0 + pre * (1.0 - sig))
         feats = dot(hidden, w_out_ref[...]).astype(BF16)
         feat_ref[2 * d] = feats[:BS]
         feat_ref[2 * d + 1] = feats[BS:]
+        for b in range(BPD):
+            wresp_ref[2 * d + b] = win_ref[d, ROWS + 16 * b : ROWS + 16 * (b + 1), :]
 
     forward(0)
 
@@ -338,10 +353,16 @@
         delta = sq / (2.0 - sq)
     both = range(BPD)
     places = [member_windows(me, home_ref, ids_ref, cnt_ref, s) for s in both]
-    for c in copies:
+    three = []
+    for q, cut in enumerate(cuts):
+        two[q].wait()
+        three.append(shift(2, 3, cut, 4 + q, 1))
+    forward(2)
+    one.wait()
+    forward(1)
+    for c in three:
         c.wait()
-    for d in range(1, WIN + 1):
-        forward(d)
+    forward(3)
 
     for s in both:
         kernel_matrix(
@@ -387,7 +408,7 @@
         back = dot(hi, w_out_ref[...], NT) + dot(lo, w_out_ref[...], NT)
         dpre = back * dsil_ref[d]
         w_out_part = w_out_part + dot(hid_ref[d], lanes(hi, lo), TN)
-        w_in_part = w_in_part + dot(win_ref[d], lanes(*split2(dpre)), TN)
+        w_in_part = w_in_part + dot(win_ref[d, :ROWS, :], lanes(*split2(dpre)), TN)
         b_part = b_part + jnp.sum(dpre, axis=0, keepdims=True)
     w_in_part = w_in_part[:, :H] + w_in_part[:, H:]
     w_out_part = w_out_part[:, :H] + w_out_part[:, H:]
@@ -432,11 +453,18 @@
     acc = red_in[0]
     for c in range(1, DEPTH):
         acc = acc + red_in[c]
-    gath[ga] = acc[:CHUNK].astype(BF16)
+    mine_ref[...] = acc[:CHUNK].astype(BF16)
     ext_ref[...] = acc[CHUNK:]
     copies = []
     for k in range(1, GROUP):
-        copies.append(send(gath.at[ga], gath.at[ga], s3.at[k], r3.at[k], mate_a(k)[1]))
+        copies.append(send(mine_ref, gath.at[ga], s3.at[k], r3.at[k], mate_a(k)[1]))
+    stores = [
+        pltpu.make_async_copy(mine_ref, gath.at[ga], out_sem.at[0]),
+        pltpu.make_async_copy(ext_ref, ext_out, out_sem.at[1]),
+        pltpu.make_async_copy(fg_ref, fg_out, out_sem.at[2]),
+    ]
+    stores[0].start()
+    stores[1].start()
 
     @pl.when(dev >= 0)
     def _():
@@ -453,7 +481,8 @@
     perm = one_hot(ps_ref[...].reshape(1, ROWS), ROWS, 0)
     pairs = dot(perm, lanes(*split2(grad)), TN)
     fg_ref[...] = pairs[:, :H] + pairs[:, H:]
-    for c in copies:
+    stores[2].start()
+    for c in copies + stores:
         c.wait()
 
 
@@ -473,6 +502,7 @@
 
 VM = pl.BlockSpec(memory_space=pltpu.VMEM)
 SM = pl.BlockSpec(memory_space=pltpu.SMEM)
+ANY = pl.BlockSpec(memory_space=pl.ANY)
 DMA = pltpu.SemaphoreType.DMA
 
 
@@ -487,10 +517,21 @@
             jax.ShapeDtypeStruct((GROUP, CHUNK, H), BF16),
             jax.ShapeDtypeStruct((8, H), F32),
         ),
-        in_specs=[VM] * 6 + [SM] * 4,
-        out_specs=(SM, VM, VM, VM),
+        in_specs=[ANY] * 6 + [SM] * 4,
+        out_specs=(SM, ANY, ANY, ANY),
         scratch_shapes=[
-            pltpu.VMEM((WIN + 1, ROWS, H), BF16),
+            pltpu.VMEM((ROWS, H), BF16),
+            pltpu.VMEM((ROWS,), BF16),
+            pltpu.VMEM((ROWS,), jnp.int32),
+            pltpu.VMEM((H, H), BF16),
+            pltpu.VMEM((H,), F32),
+            pltpu.VMEM((H, H), BF16),
+            pltpu.VMEM((ROWS, H), F32),
+            pltpu.VMEM((CHUNK, H), BF16),
+            pltpu.VMEM((8, H), F32),
+            DMA((6,)),
+            DMA((3,)),
+            pltpu.VMEM((WIN + 1, ROWS + 32, H), BF16),
             pltpu.VMEM(((WIN + 1) * BPD, 16, H), BF16),
             pltpu.VMEM(((WIN + 1) * BPD, BS, H), BF16),
             pltpu.VMEM((WIN + 1, ROWS, H), BF16),
@@ -508,7 +549,8 @@
             pltpu.VMEM((BPD, BS, B), F32),
             pltpu.VMEM((BPD, 8, B), F32),
         ]
-        + [DMA((WIN + 1,))] * 6
+        + [DMA((8,))] * 2
+        + [DMA((WIN + 1,))] * 2
         + [DMA((GROUP,))] * 6
         + [DMA, DMA],
         compiler_params=pltpu.CompilerParams(

time: 55.9 us -> 54.9 us (0.982)
  Pallas kernels: 54.9 us -> 53.9 us
    pallas_call x1, Pallas kernels: 53.2 us -> 52.3 us  [shards(): pl.pallas_call(main_kernel, out_shape=(jax.ShapeDtypeStruct((BPD,), F32),...]
where the time goes in v4:
time: 54.9 us; the launch traced here: 54.7 us
  Pallas kernels  53.9 us (98%)
  between operations  0.8 us (1%)
    pallas_call x1, Pallas kernels, shards(): pl.pallas_call(main_kernel, out_shape=(jax.ShapeDtypeStruct((BPD,), F32),...  52.3 us
    pallas_call x1, Pallas kernels, shards(): pl.pallas_call(finish_kernel, out_shape=(jax.ShapeDtypeStruct((BPD,), F32...  1.65 us

profile of v4, /device:TPU:1, one launch (start us, length us, event | category | flops | bytes accessed | tf_op | source)
XLA Modules:
  0.0 54.7 jit_solution(13171346086689277729)
XLA Ops:
  0.6 52.3 %vecchia_main.1 = (f32[2]{0:T(128)}, f32[192,128]{1,0:T(8,128)}, bf16[16,16,128]{2,1,0:T(8,128)(2,1)}, f32[8,128]{1,0:T(8,128)}) custom-call(bf16[192,128]{1,0:T(8,128)(2,1)} %x_in.1, bf16[192]{0:T(256)(128)(2,1)} %resp_in.1, s32[192]{0:T(256)} %ps_in.1, bf16[128,128]{1,0:T(8,128)(2,1)} %w_in_in.1, f32[128]{0:T(128)} %b_in.1, bf16[128,128]{1,0:T(8,128)(2,1)} %w_out_in.1, ...), custom_call_target="tpu_custom_call" | custom-call | tf_op jit(solution)/shard_map/vecchia_main/pallas_call | solution.py:512
  52.9 1.7 %vecchia_finish.1 = (f32[2]{0:T(128)}, f32[192,128]{1,0:T(8,128)}, f32[128,128]{1,0:T(8,128)}, f32[128]{0:T(128)}, f32[128,128]{1,0:T(8,128)}, /*index=5*/f32[3]{0:T(128)}) custom-call(f32[2]{0:T(128)} %get-tuple-element.10.ll_in, f32[192,128]{1,0:T(8,128)} %get-tuple-element.11.grad_ref, bf16[16,16,128]{2,1,0:T(8,128)(2,1)} %get-tuple-element.12.gath_ref, ...), custom_call_target="tpu_custom_call" | custom-call | tf_op jit(solution)/shard_map/vecchia_finish/pallas_call | solution.py:564

commit v5 on v4

--- a/solution.py
+++ b/solution.py
@@ -56,8 +56,8 @@
 
 
 def mul2(a, b):
-    n = b.shape[1]
-    pair = lanes(*split2(b))
+    n = (b[0] if isinstance(b, tuple) else b).shape[1]
+    pair = lanes(*(b if isinstance(b, tuple) else split2(b)))
     out = dot(lanes(*split2(a)), rows_of(pair, pair))
     return out[:, :n] + out[:, n:]
 
@@ -88,24 +88,24 @@
     ).astype(F32)
 
 
-def inverses(mats, eye, coef, scales, below=None):
+def inverses(mats, eye, scan, fill=()):
+    coef, scales = scan
+    fill = list(fill)
+    share = -(-len(fill) // (STEPS - 2)) if fill else 0
     res = [eye - coef * a for a in mats]
     inv = [(scales[0] * coef) * (eye + r) for r in res]
     res = [(1.0 - scales[0]) * eye + scales[0] * mul3(r, r) for r in res]
     for j in range(1, STEPS - 1):
         s = scales[j]
-        both = [mul3(rows_of(r, x), r) for x, r in zip(inv, res)]
-        if below is not None and j == STEPS - 2:
-            panel = [mul3(b, x) for b, x in zip(below, inv)]
-            panel = [s * (p + mul3(p, r)) for p, r in zip(panel, res)]
+        mul = mul2 if j == STEPS - 2 else mul3
+        both = [mul(rows_of(r, x), r) for x, r in zip(inv, res)]
+        for work in fill[:share]:
+            work()
+        fill = fill[share:]
         inv = [s * (x + b[B:]) for x, b in zip(inv, both)]
         res = [(1.0 - s) * eye + s * b[:B] for b in both]
     s = scales[-1]
-    parts = [split3(r) for r in res]
-    if below is not None:
-        panel = [s * (p + mul3(p, r)) for p, r in zip(panel, parts)]
-    inv = [s * (x + mul3(x, r)) for x, r in zip(inv, parts)]
-    return inv if below is None else (inv, panel)
+    return [s * x for x in inv], res
 
 
 def device(index):
@@ -143,7 +143,7 @@
     return places
 
 
-def kernel_matrix(s, count, places, feat_ref, resp_ref, z_ref, e_ref, k_ref, inv_sq, var, nug, eye):
+def kernel_rows(s, count, places, feat_ref, resp_ref, z_ref, e_ref, k_ref, inv_sq, var, nug, eye):
     lane1 = lax.broadcasted_iota(jnp.int32, (1, B), 1)
     y_row = jnp.zeros((1, N), F32)
     for k, (w, flag) in enumerate(places + [(s, None)]):
@@ -158,41 +158,46 @@
     z_ref[s, (NMAX + 1) * BS :, :] = jnp.zeros((N - (NMAX + 1) * BS, H), BF16)
     z = z_ref[s]
     gram = dot(z, z, NT)
+    e_ref[s] = gram
     diag = [jnp.where(eye > 0.0, gram[i * B : (i + 1) * B, i * B : (i + 1) * B], 0.0) for i in range(4)]
     sq_row = lanes(*[jnp.sum(d, axis=0, keepdims=True) for d in diag])
+    sq_col = [jnp.sum(d, axis=1, keepdims=True) for d in diag]
     col_id = lax.broadcasted_iota(jnp.int32, (1, N), 1)
     own = (col_id >= NMAX * BS) & (col_id < (NMAX + 1) * BS)
     v_row = jnp.where((col_id < count * BS) | own, 1.0, 0.0)
-    for i in range(4):
-        row_id = lax.broadcasted_iota(jnp.int32, (B, 1), 0) + i * B
+
+    def piece(i, c):
+        part = slice(c, c + 32)
+        out = slice(i * B + c, i * B + c + 32)
+        row_id = lax.broadcasted_iota(jnp.int32, (32, 1), 0) + (i * B + c)
         own = (row_id >= NMAX * BS) & (row_id < (NMAX + 1) * BS)
         v_col = jnp.where((row_id < count * BS) | own, 1.0, 0.0)
-        sq_col = jnp.sum(diag[i], axis=1, keepdims=True)
-        mine = slice(i * B, (i + 1) * B)
-        for c in range(0, B, 32):
-            part = slice(c, c + 32)
-            out = slice(i * B + c, i * B + c + 32)
-            d2 = jnp.maximum(sq_col[part] + sq_row - 2.0 * gram[out], 0.0)
-            r2 = d2 * inv_sq + 1e-06
-            rad = SQRT_THREE * (r2 * lax.rsqrt(r2))
-            e = jnp.exp(-rad) * (v_col[part] * v_row)
-            e_ref[s, out, :] = e
-            wide = (i + 1) * B
-            kern = var * (1.0 + rad[:, :wide]) * e[:, :wide]
-            spot = kern[:, i * B :] + eye[part] * (nug * v_col[part] + 1.0 - v_col[part])
-            k_ref[s, out, :wide] = lanes(kern[:, : i * B], spot) if i else spot
-    k_ref[s, 3 * B + BS : 3 * B + BS + 1, :] = y_row
-
-
-def eliminate(both, k_ref, eye, coef, scales):
+        d2 = jnp.maximum(sq_col[i][part] + sq_row - 2.0 * e_ref[s, out, :], 0.0)
+        r2 = d2 * inv_sq + 1e-06
+        rad = SQRT_THREE * (r2 * lax.rsqrt(r2))
+        e = jnp.exp(-rad) * (v_col * v_row)
+        e_ref[s, out, :] = e
+        wide = (i + 1) * B
+        kern = var * (1.0 + rad[:, :wide]) * e[:, :wide]
+        spot = kern[:, i * B :] + eye[part] * (nug * v_col + 1.0 - v_col)
+        k_ref[s, out, :wide] = lanes(kern[:, : i * B], spot) if i else spot
+        if i == 3 and c == BS:
+            k_ref[s, 3 * B + BS : 3 * B + BS + 1, :] = y_row
+
+    return [[lambda i=i, c=c: piece(i, c) for c in range(0, B, 32)] for i in range(4)]
+
+
+def eliminate(both, k_ref, eye, scan, fill):
     invs = []
     for i in range(3):
         lo = (i + 1) * B
         cols = slice(i * B, lo)
+        x, r = inverses([block(k_ref, s, i, i) for s in both], eye, scan, fill)
+        fill = []
         below = [split3(k_ref[s, lo:, cols]) for s in both]
-        cur, panel = inverses([block(k_ref, s, i, i) for s in both], eye, coef, scales, below)
-        invs.append([split3(c) for c in cur])
-        panel = [split3(p) for p in panel]
+        panel = [mul3(below[s], x[s]) for s in both]
+        panel = [split3(panel[s] + mul2(panel[s], r[s])) for s in both]
+        invs.append([split3(x[s] + mul2(x[s], r[s])) for s in both])
         for b in range(i + 1, 4):
             first = (b - i - 1) * B
             for s in both:
@@ -200,45 +205,73 @@
                 k_ref[s, b * B :, at] = k_ref[s, b * B :, at] - mul3_nt(
                     tuple(p[first:] for p in panel[s]), tuple(p[first : first + B] for p in below[s])
                 )
-    return invs
-
-
-def joint_gradient(s, invs, s_inv, resid, z_ref, e_ref, k_ref, var, inv_sq, nug, eye, real):
+    return invs, [block(k_ref, s, 3, 3) for s in both], []
+
+
+def joint_gradients(both, invs, schur, resid, scan, fill, z_ref, e_ref, k_ref, var, inv_sq, nug, eye, real):
     sub = lax.broadcasted_iota(jnp.int32, (B, B), 0)
     lane = lax.broadcasted_iota(jnp.int32, (B, B), 1)
-    x3 = mul3(block(k_ref, s, 3, 2), invs[2][s])
-    p3 = split3(x3)
-    x2 = mul3(block(k_ref, s, 3, 1) - mul3(p3, block(k_ref, s, 2, 1)), invs[1][s])
-    p2 = split3(x2)
-    t1 = block(k_ref, s, 3, 0) - mul3(p3, block(k_ref, s, 2, 0)) - mul3(p2, block(k_ref, s, 1, 0))
-    x1 = mul3(t1, invs[0][s])
+    lane1 = lax.broadcasted_iota(jnp.int32, (1, B), 1)
     sign = jnp.where(lax.broadcasted_iota(jnp.int32, (B, 1), 0) < BS, -1.0, 1.0)
-    ys = [x1 * sign, x2 * sign, x3 * sign]
+    p3, p2, t1, x1, ys, w_pair = {}, {}, {}, {}, {}, {}
+
+    def back(s, step):
+        if step == 0:
+            p3[s] = split3(mul3(block(k_ref, s, 3, 2), invs[2][s]))
+        elif step == 1:
+            p2[s] = block(k_ref, s, 3, 1) - mul3(p3[s], block(k_ref, s, 2, 1))
+            t1[s] = block(k_ref, s, 3, 0) - mul3(p3[s], block(k_ref, s, 2, 0))
+        elif step == 2:
+            p2[s] = split3(mul3(p2[s], invs[1][s]))
+        elif step == 3:
+            t1[s] = t1[s] - mul3(p2[s], block(k_ref, s, 1, 0))
+        elif step == 4:
+            x1[s] = mul3(t1[s], invs[0][s])
+        else:
+            x2, x3 = [p[0].astype(F32) + (p[1].astype(F32) + p[2].astype(F32)) for p in (p2[s], p3[s])]
+            ys[s] = lanes(x1[s] * sign, x2 * sign, x3 * sign)
+            w = rows_of(*[ys[s][:, i * B : (i + 1) * B].T for i in range(3)])
+            w_pair[s] = lanes(*split2(w))
+
     own = jnp.where(real, eye, 0.0)
-    beta_m = mul3(resid, s_inv)
-    beta_row = beta_m[BS : BS + 1]
-    beta_col = jnp.sum(eye * beta_row, axis=1, keepdims=True)
-    mid = jnp.where(real, beta_col * beta_row - s_inv, 0.0) + beta_m
-    mid = mid + jnp.where((lane == BS) & (sub < BS), beta_col, 0.0)
-    quad = jnp.sum(jnp.sum(resid * beta_m, axis=0, keepdims=True), axis=1, keepdims=True)
-    y = lanes(*ys, own)
-    prod = mul2(mid, y)
-    trace = jnp.sum(jnp.sum(prod * y, axis=0, keepdims=True), axis=1, keepdims=True)
-    t2 = 0.5 * nug * trace
-    t1 = 0.5 * quad - 0.5 * BS - t2
-    w = rows_of(*[m.T for m in ys])
-    g = mul2(w, prod)
-    low = jnp.where(lax.broadcasted_iota(jnp.int32, (B, 1), 0) < BS, prod, 0.0)
-    high, rest = split2(rows_of(g * e_ref[s, : 3 * B, :], low * e_ref[s, 3 * B :, :]))
-    z = z_ref[s]
-    rhs = lanes(z, jnp.ones_like(z))
-    pz = dot(high, rhs) + dot(rest, rhs)
-    zf = z.astype(F32)
-    grad = (3.0 * var * inv_sq) * (pz[:, :H] - pz[:, H:] * zf)
-    t0 = -jnp.sum(jnp.sum(grad * zf, axis=0, keepdims=True), axis=1, keepdims=True)
-    lane1 = lax.broadcasted_iota(jnp.int32, (1, B), 1)
-    hyper = jnp.where(lane1 == 0, t0, 0.0) + jnp.where(lane1 == 1, t1, 0.0)
-    return grad, hyper + jnp.where(lane1 == 2, t2, 0.0), quad
+    steps = [lambda s=s, step=step: back(s, step) for step in range(6) for s in both]
+    x, r = inverses(schur, eye, scan, fill + steps)
+    beta_m = [mul3(resid[s], x[s]) for s in both]
+    beta_m = [beta_m[s] + mul2(beta_m[s], r[s]) for s in both]
+    s_inv = [x[s] + mul2(x[s], r[s]) for s in both]
+    y_parts = [split2(lanes(ys[s], own)) for s in both]
+    beta_row = [m[BS : BS + 1] for m in beta_m]
+    beta_col = [jnp.sum(eye * b, axis=1, keepdims=True) for b in beta_row]
+    mid = [
+        jnp.where(real, beta_col[s] * beta_row[s] - s_inv[s], 0.0)
+        + beta_m[s]
+        + jnp.where((lane == BS) & (sub < BS), beta_col[s], 0.0)
+        for s in both
+    ]
+    prod = [mul2(mid[s], y_parts[s]) for s in both]
+    pairs = [lanes(*split2(p)) for p in prod]
+    g = [dot(w_pair[s], rows_of(pairs[s], pairs[s])) for s in both]
+    below = lax.broadcasted_iota(jnp.int32, (B, 1), 0) < BS
+    low = [jnp.where(below, prod[s], 0.0) for s in both]
+    weights = [
+        split2(rows_of((g[s][:, :N] + g[s][:, N:]) * e_ref[s, : 3 * B, :], low[s] * e_ref[s, 3 * B :, :]))
+        for s in both
+    ]
+    rhs = [lanes(z_ref[s], jnp.ones((N, H), BF16)) for s in both]
+    pz = [dot(weights[s][0], rhs[s]) + dot(weights[s][1], rhs[s]) for s in both]
+    out = []
+    for s in both:
+        quad = jnp.sum(jnp.sum(resid[s] * beta_m[s], axis=0, keepdims=True), axis=1, keepdims=True)
+        y = lanes(ys[s], own)
+        trace = jnp.sum(jnp.sum(prod[s] * y, axis=0, keepdims=True), axis=1, keepdims=True)
+        t2 = 0.5 * nug * trace
+        t1 = 0.5 * quad - 0.5 * BS - t2
+        zf = z_ref[s].astype(F32)
+        grad = (3.0 * var * inv_sq) * (pz[s][:, :H] - pz[s][:, H:] * zf)
+        t0 = -jnp.sum(jnp.sum(grad * zf, axis=0, keepdims=True), axis=1, keepdims=True)
+        hyper = jnp.where(lane1 == 0, t0, 0.0) + jnp.where(lane1 == 1, t1, 0.0)
+        out.append((grad, hyper + jnp.where(lane1 == 2, t2, 0.0), quad))
+    return out
 
 
 def pivot_steps(mat_ref, log_ref, first, last):
@@ -261,10 +294,10 @@
 
 
 def main_kernel(
-    x_in, resp_in, ps_in, w_in_in, b_in, w_out_in, home_ref, ids_ref, cnt_ref, par_ref,
-    ll_ref, fg_out, gath, ext_out,
-    x_ref, resp_ref, ps_ref, w_in_ref, b_ref, w_out_ref,
-    fg_ref, mine_ref, ext_ref, in_sem, out_sem,
+    x_in, resp_in, ps_in, w_in_in, b_in, w_out_in, home_in, ids_in, cnt_in, par_in,
+    ll_ref, hyp_ref, fg_out, gath, b_out,
+    x_ref, resp_ref, ps_ref, w_in_ref, b_ref, w_out_ref, home_ref, ids_ref, cnt_ref, par_ref,
+    fg_ref, mine_ref, bsum_ref, in_sem, out_sem,
     win_ref, wresp_ref, feat_ref, hid_ref, dsil_ref, z_ref, e_ref, k_ref, gw_ref,
     out_buf, in_buf, part, part_in, pair, red_in, mat_ref, log_ref,
     f_send, f_recv, g_send, g_recv, s1, r1, s2, r2, s3, r3, c_send, c_recv,
@@ -289,8 +322,8 @@
     def later(k):
         return device(lax.rem(me + k + total, total))
 
-    ops = (x_in, resp_in, ps_in, w_in_in, b_in, w_out_in)
-    refs = (x_ref, resp_ref, ps_ref, w_in_ref, b_ref, w_out_ref)
+    ops = (x_in, resp_in, ps_in, w_in_in, b_in, w_out_in, home_in, ids_in, cnt_in, par_in)
+    refs = (x_ref, resp_ref, ps_ref, w_in_ref, b_ref, w_out_ref, home_ref, ids_ref, cnt_ref, par_ref)
     loads = [pltpu.make_async_copy(a, b, in_sem.at[i]) for i, (a, b) in enumerate(zip(ops, refs))]
     for c in loads:
         c.start()
@@ -364,26 +397,27 @@
         c.wait()
     forward(3)
 
-    for s in both:
-        kernel_matrix(
+    rows = [
+        kernel_rows(
             s, cnt_ref[s], places[s], feat_ref, wresp_ref, z_ref, e_ref, k_ref, inv_sq, var, nug, eye
         )
-    invs = eliminate(both, k_ref, eye, coef, scales)
+        for s in both
+    ]
+    for s in both:
+        for work in rows[s][0]:
+            work()
+    fill = [work for i in range(1, 4) for s in both for work in rows[s][i]]
+    scan = (coef, scales)
+    invs, last, fill = eliminate(both, k_ref, eye, scan, fill)
     real = (lane < BS) & (sub < BS)
-    last = [block(k_ref, s, 3, 3) for s in both]
     resid = [jnp.where((sub == BS) & (lane < BS), m, 0.0) for m in last]
     schur = [jnp.where(real, m, eye) for m in last]
-    s_inv = inverses(schur, eye, coef, scales)
     for s in both:
         mat_ref[s] = schur[s][:BS]
-    grads, hypers, quads = [], [], []
-    for s in both:
-        grad, hyper, quad = joint_gradient(
-            s, invs, s_inv[s], resid[s], z_ref, e_ref, k_ref, var, inv_sq, nug, eye, real
-        )
-        grads.append(grad)
-        hypers.append(hyper)
-        quads.append(quad)
+    found = joint_gradients(
+        both, invs, schur, resid, scan, fill, z_ref, e_ref, k_ref, var, inv_sq, nug, eye, real
+    )
+    grads, hypers, quads = [list(part) for part in zip(*found)]
     for w in range((WIN + 1) * BPD):
         acc = grads[w][NMAX * BS : (NMAX + 1) * BS] if w < BPD else jnp.zeros((BS, H), F32)
         for s in both:
@@ -453,14 +487,16 @@
     acc = red_in[0]
     for c in range(1, DEPTH):
         acc = acc + red_in[c]
-    mine_ref[...] = acc[:CHUNK].astype(BF16)
-    ext_ref[...] = acc[CHUNK:]
+    acc = acc * (1.0 / (total * ROWS))
+    mine_ref[...] = acc[:CHUNK]
+    bsum_ref[...] = acc[CHUNK : CHUNK + 1].reshape(H)
+    place = pl.ds(pl.multiple_of(ga * CHUNK, CHUNK), CHUNK)
     copies = []
     for k in range(1, GROUP):
-        copies.append(send(mine_ref, gath.at[ga], s3.at[k], r3.at[k], mate_a(k)[1]))
+        copies.append(send(mine_ref, gath.at[place], s3.at[k], r3.at[k], mate_a(k)[1]))
     stores = [
-        pltpu.make_async_copy(mine_ref, gath.at[ga], out_sem.at[0]),
-        pltpu.make_async_copy(ext_ref, ext_out, out_sem.at[1]),
+        pltpu.make_async_copy(mine_ref, gath.at[place], out_sem.at[0]),
+        pltpu.make_async_copy(bsum_ref, b_out, out_sem.at[1]),
         pltpu.make_async_copy(fg_ref, fg_out, out_sem.at[2]),
     ]
     stores[0].start()
@@ -472,6 +508,8 @@
         for s in both:
             ll = -0.5 * (log_ref[s, 0:1, 0:1] + log_ref[s, 1:2, 0:1]) * (1.0 / BS) - 0.5 * LOG_TWO_PI
             ll_ref[s] = jnp.sum(ll)
+        for i in range(3):
+            hyp_ref[i] = jnp.sum(acc[CHUNK + 1 : CHUNK + 2, i : i + 1])
 
     for c in returns:
         c.wait()
@@ -486,18 +524,15 @@
         c.wait()
 
 
-def finish_kernel(ll_in, grad_ref, gath_ref, ext_ref, ll_ref, fg_ref, gin_ref, b_ref, gout_ref, hyp_ref):
-    scale = 1.0 / (lax.axis_size("region") * lax.axis_size("dev") * ROWS)
-    fg_ref[...] = grad_ref[...]
-    for c in range(8):
-        gin_ref[c * CHUNK : (c + 1) * CHUNK, :] = gath_ref[c].astype(F32) * scale
-        gout_ref[c * CHUNK : (c + 1) * CHUNK, :] = gath_ref[8 + c].astype(F32) * scale
-    ext = ext_ref[...] * scale
-    b_ref[...] = ext[0:1].reshape(H)
+def finish_kernel(ll_in, hyp_in, grad_in, weights_in, b_in, ll_out, fg_out, gin_out, b_out, gout_out, hyp_out):
+    fg_out[...] = grad_in[...]
+    gin_out[...] = weights_in[:H, :]
+    gout_out[...] = weights_in[H:, :]
+    b_out[...] = b_in[...]
+    for s in range(BPD):
+        ll_out[s] = ll_in[s]
     for i in range(3):
-        hyp_ref[i] = jnp.sum(ext[1:2, i : i + 1])
-    for s in range(BPD):
-        ll_ref[s] = ll_in[s]
+        hyp_out[i] = hyp_in[i]
 
 
 VM = pl.BlockSpec(memory_space=pltpu.VMEM)
@@ -509,16 +544,17 @@
 def shards(
     inputs, responses, point_slot, block_home, nbr_ids, nbr_count, w_in, b_in, w_out, kernel_params
 ):
-    loglik, grad, gath, ext = pl.pallas_call(
+    loglik, hyper, grad, weights, bias = pl.pallas_call(
         main_kernel,
         out_shape=(
             jax.ShapeDtypeStruct((BPD,), F32),
+            jax.ShapeDtypeStruct((3,), F32),
             jax.ShapeDtypeStruct((ROWS, H), F32),
-            jax.ShapeDtypeStruct((GROUP, CHUNK, H), BF16),
-            jax.ShapeDtypeStruct((8, H), F32),
+            jax.ShapeDtypeStruct((GROUP * CHUNK, H), F32),
+            jax.ShapeDtypeStruct((H,), F32),
         ),
-        in_specs=[ANY] * 6 + [SM] * 4,
-        out_specs=(SM, ANY, ANY, ANY),
+        in_specs=[ANY] * 10,
+        out_specs=(SM, SM, ANY, ANY, ANY),
         scratch_shapes=[
             pltpu.VMEM((ROWS, H), BF16),
             pltpu.VMEM((ROWS,), BF16),
@@ -526,10 +562,14 @@
             pltpu.VMEM((H, H), BF16),
             pltpu.VMEM((H,), F32),
             pltpu.VMEM((H, H), BF16),
+            pltpu.SMEM(block_home.shape, jnp.int32),
+            pltpu.SMEM((BPD, NMAX), jnp.int32),
+            pltpu.SMEM((BPD,), jnp.int32),
+            pltpu.SMEM((3,), F32),
             pltpu.VMEM((ROWS, H), F32),
-            pltpu.VMEM((CHUNK, H), BF16),
-            pltpu.VMEM((8, H), F32),
-            DMA((6,)),
+            pltpu.VMEM((CHUNK, H), F32),
+            pltpu.VMEM((H,), F32),
+            DMA((10,)),
             DMA((3,)),
             pltpu.VMEM((WIN + 1, ROWS + 32, H), BF16),
             pltpu.VMEM(((WIN + 1) * BPD, 16, H), BF16),
@@ -571,10 +611,10 @@
             jax.ShapeDtypeStruct((H, H), F32),
             jax.ShapeDtypeStruct((3,), F32),
         ),
-        in_specs=[SM, VM, VM, VM],
+        in_specs=[SM, SM, VM, VM, VM],
         out_specs=(SM, VM, VM, VM, VM, SM),
         name="vecchia_finish",
-    )(loglik, grad, gath, ext)
+    )(loglik, hyper, grad, weights, bias)
     return loglik, feature_grad, g_in, g_b, g_out, hyper
 
 

time: 54.9 us -> 52.1 us (0.949)
  Pallas kernels: 53.9 us -> 51.1 us
    pallas_call x1, Pallas kernels: 52.3 us -> 49.4 us  [shards(): pl.pallas_call(main_kernel, out_shape=(jax.ShapeDtypeStruct((BPD,), F32),...]
where the time goes in v5:
time: 52.1 us; the launch traced here: 51.9 us
  Pallas kernels  51.1 us (98%)
  between operations  0.8 us (2%)
    pallas_call x1, Pallas kernels, shards(): pl.pallas_call(main_kernel, out_shape=(jax.ShapeDtypeStruct((BPD,), F32),...  49.4 us
    pallas_call x1, Pallas kernels, shards(): pl.pallas_call(finish_kernel, out_shape=(jax.ShapeDtypeStruct((BPD,), F32...  1.67 us

profile of v5, /device:TPU:1, one launch (start us, length us, event | category | flops | bytes accessed | tf_op | source)
XLA Modules:
  0.0 51.9 jit_solution(1033726378581919766)
XLA Ops:
  0.6 49.4 %vecchia_main.1 = (f32[2]{0:T(128)}, f32[3]{0:T(128)}, f32[192,128]{1,0:T(8,128)}, f32[256,128]{1,0:T(8,128)}, f32[128]{0:T(128)}) custom-call(bf16[192,128]{1,0:T(8,128)(2,1)} %x_in.1, bf16[192]{0:T(256)(128)(2,1)} %resp_in.1, s32[192]{0:T(256)} %ps_in.1, bf16[128,128]{1,0:T(8,128)(2,1)} %w_in_in.1, f32[128]{0:T(128)} %b_in.1, bf16[128,128]{1,0:T(8,128)(2,1)} %w_out_in.1, ...), custom_call_target="tpu_custom_call" | custom-call | tf_op jit(solution)/shard_map/vecchia_main/pallas_call | solution.py:547
  50.1 1.7 %vecchia_finish.1 = (f32[2]{0:T(128)}, f32[192,128]{1,0:T(8,128)}, f32[128,128]{1,0:T(8,128)}, f32[128]{0:T(128)}, f32[128,128]{1,0:T(8,128)}, /*index=5*/f32[3]{0:T(128)}) custom-call(f32[2]{0:T(128)} %get-tuple-element.11.ll_in, f32[3]{0:T(128)} %get-tuple-element.12.hyp_in, f32[192,128]{1,0:T(8,128)} %get-tuple-element.13.grad_in, ...), custom_call_target="tpu_custom_call" | custom-call | tf_op jit(solution)/shard_map/vecchia_finish/pallas_call | solution.py:604

commit v6 on v5

--- a/solution.py
+++ b/solution.py
@@ -110,7 +110,7 @@
 
 def device(index):
     per = lax.axis_size("dev")
-    return (index // per, index % per)
+    return (lax.div(index, per), lax.rem(index, per))
 
 
 def my_index():
@@ -305,12 +305,16 @@
     total = lax.axis_size("region") * lax.axis_size("dev")
     region, dev = lax.axis_index("region"), lax.axis_index("dev")
     me = my_index()
-    x, core, y, z = region // 2, region % 2, dev // DEPTH, dev % DEPTH
+    x, core = lax.div(region, 2), lax.rem(region, 2)
+    y, z = lax.div(dev, DEPTH), lax.rem(dev, DEPTH)
     ga = x * 4 + y
 
-    def mate_a(k):
-        other = lax.rem(ga + k, GROUP)
-        return other, ((other // 4) * 2 + core, (other % 4) * DEPTH + z)
+    xs = [x] + [lax.rem(x + k, 4) for k in range(1, 4)]
+    ys = [y] + [lax.rem(y + k, 4) for k in range(1, 4)]
+    mates = [
+        (xs[k // 4] * 4 + ys[k % 4], (xs[k // 4] * 2 + core, ys[k % 4] * DEPTH + z)) for k in range(GROUP)
+    ]
+    column = [(region, y * DEPTH + lax.rem(z + k, DEPTH)) for k in range(DEPTH)]
 
     def send(src, dst, ssem, rsem, place):
         copy = pltpu.make_async_remote_copy(
@@ -332,10 +336,9 @@
         pl.semaphore_signal(barrier, inc=1, device_id=later(k), device_id_type=MESH)
         pl.semaphore_signal(barrier, inc=1, device_id=later(-k), device_id_type=MESH)
     for k in range(1, GROUP):
-        pl.semaphore_signal(barrier, inc=1, device_id=mate_a(k)[1], device_id_type=MESH)
+        pl.semaphore_signal(barrier, inc=1, device_id=mates[k][1], device_id_type=MESH)
     for k in range(1, DEPTH):
-        place = (region, y * DEPTH + lax.rem(z + k, DEPTH))
-        pl.semaphore_signal(barrier, inc=1, device_id=place, device_id_type=MESH)
+        pl.semaphore_signal(barrier, inc=1, device_id=column[k], device_id_type=MESH)
     pl.semaphore_signal(barrier, inc=1, device_id=(x * 2 + 1 - core, dev), device_id_type=MESH)
 
     for c in loads:
@@ -447,16 +450,29 @@
     w_in_part = w_in_part[:, :H] + w_in_part[:, H:]
     w_out_part = w_out_part[:, :H] + w_out_part[:, H:]
     row8 = lax.broadcasted_iota(jnp.int32, (8, H), 0)
+    row16 = lax.broadcasted_iota(jnp.int32, (CHUNK, H), 0)
+
+    def pack(bias, hyper):
+        tile = jnp.zeros((CHUNK, H), F32)
+        for i, one_row in enumerate(split2(bias) + split2(hyper)):
+            tile = tile + jnp.where(row16 == i, one_row.astype(F32), 0.0)
+        return tile.astype(BF16)
+
+    def unpack(tile):
+        return tile[0:1] + tile[1:2], tile[2:3] + tile[3:4]
+
     for s in both:
         log_ref[s] = jnp.where(row8 == 1, quads[s], 0.0)
-    small = jnp.where(row8 == 0, b_part, 0.0) + jnp.where(row8 == 1, hypers[0] + hypers[1], 0.0)
+    small = pack(b_part, hypers[0] + hypers[1])
+    w_in_part = w_in_part.astype(BF16)
+    w_out_part = w_out_part.astype(BF16)
     for c in range(GROUP):
         src = w_in_part if c < 8 else w_out_part
         part[c, :CHUNK, :] = src[(c % 8) * CHUNK : (c % 8 + 1) * CHUNK]
         part[c, CHUNK:, :] = small
     copies = []
     for k in range(1, GROUP):
-        other, place = mate_a(k)
+        other, place = mates[k]
         copies.append(send(part.at[other], part_in.at[ga], s1.at[k], r1.at[k], place))
     part_in[ga] = part[ga]
 
@@ -466,17 +482,20 @@
 
     for c in copies:
         c.wait()
-    acc = part_in[0]
+    acc = part_in[0].astype(F32)
     for c in range(1, GROUP):
-        acc = acc + part_in[c]
-    pair[core] = acc
+        acc = acc + part_in[c].astype(F32)
+    bias, hyper = unpack(acc[CHUNK:])
+    pair[core, :CHUNK, :] = acc[:CHUNK]
+    pair[core, CHUNK:, :] = jnp.where(row8 == 0, bias, 0.0) + jnp.where(row8 == 1, hyper, 0.0)
     copy = send(pair.at[core], pair.at[core], c_send, c_recv, (x * 2 + 1 - core, dev))
     copy.wait()
-    red_in[z] = pair[0] + pair[1]
+    acc = pair[0] + pair[1]
+    red_in[z, :CHUNK, :] = acc[:CHUNK].astype(BF16)
+    red_in[z, CHUNK:, :] = pack(acc[CHUNK : CHUNK + 1], acc[CHUNK + 1 : CHUNK + 2])
     copies = []
     for k in range(1, DEPTH):
-        place = (region, y * DEPTH + lax.rem(z + k, DEPTH))
-        copies.append(send(red_in.at[z], red_in.at[z], s2.at[k], r2.at[k], place))
+        copies.append(send(red_in.at[z], red_in.at[z], s2.at[k], r2.at[k], column[k]))
 
     @pl.when(dev >= 0)
     def _():
@@ -484,16 +503,17 @@
 
     for c in copies:
         c.wait()
-    acc = red_in[0]
+    acc = red_in[0].astype(F32)
     for c in range(1, DEPTH):
-        acc = acc + red_in[c]
+        acc = acc + red_in[c].astype(F32)
     acc = acc * (1.0 / (total * ROWS))
-    mine_ref[...] = acc[:CHUNK]
-    bsum_ref[...] = acc[CHUNK : CHUNK + 1].reshape(H)
+    mine_ref[...] = acc[:CHUNK].astype(BF16)
+    bias, hyper = unpack(acc[CHUNK:])
+    bsum_ref[...] = bias.reshape(H)
     place = pl.ds(pl.multiple_of(ga * CHUNK, CHUNK), CHUNK)
     copies = []
     for k in range(1, GROUP):
-        copies.append(send(mine_ref, gath.at[place], s3.at[k], r3.at[k], mate_a(k)[1]))
+        copies.append(send(mine_ref, gath.at[place], s3.at[k], r3.at[k], mates[k][1]))
     stores = [
         pltpu.make_async_copy(mine_ref, gath.at[place], out_sem.at[0]),
         pltpu.make_async_copy(bsum_ref, b_out, out_sem.at[1]),
@@ -509,7 +529,7 @@
             ll = -0.5 * (log_ref[s, 0:1, 0:1] + log_ref[s, 1:2, 0:1]) * (1.0 / BS) - 0.5 * LOG_TWO_PI
             ll_ref[s] = jnp.sum(ll)
         for i in range(3):
-            hyp_ref[i] = jnp.sum(acc[CHUNK + 1 : CHUNK + 2, i : i + 1])
+            hyp_ref[i] = jnp.sum(hyper[:, i : i + 1])
 
     for c in returns:
         c.wait()
@@ -526,8 +546,8 @@
 
 def finish_kernel(ll_in, hyp_in, grad_in, weights_in, b_in, ll_out, fg_out, gin_out, b_out, gout_out, hyp_out):
     fg_out[...] = grad_in[...]
-    gin_out[...] = weights_in[:H, :]
-    gout_out[...] = weights_in[H:, :]
+    gin_out[...] = weights_in[:H, :].astype(F32)
+    gout_out[...] = weights_in[H:, :].astype(F32)
     b_out[...] = b_in[...]
     for s in range(BPD):
         ll_out[s] = ll_in[s]
@@ -550,7 +570,7 @@
             jax.ShapeDtypeStruct((BPD,), F32),
             jax.ShapeDtypeStruct((3,), F32),
             jax.ShapeDtypeStruct((ROWS, H), F32),
-            jax.ShapeDtypeStruct((GROUP * CHUNK, H), F32),
+            jax.ShapeDtypeStruct((GROUP * CHUNK, H), BF16),
             jax.ShapeDtypeStruct((H,), F32),
         ),
         in_specs=[ANY] * 10,
@@ -567,7 +587,7 @@
             pltpu.SMEM((BPD,), jnp.int32),
             pltpu.SMEM((3,), F32),
             pltpu.VMEM((ROWS, H), F32),
-            pltpu.VMEM((CHUNK, H), F32),
+            pltpu.VMEM((CHUNK, H), BF16),
             pltpu.VMEM((H,), F32),
             DMA((10,)),
             DMA((3,)),
@@ -582,10 +602,10 @@
             pltpu.VMEM(((WIN + 1) * BPD, BS, H), F32),
             pltpu.VMEM((WIN, ROWS, H), BF16),
             pltpu.VMEM((WIN, ROWS, H), BF16),
-            pltpu.VMEM((GROUP, CHUNK + 8, H), F32),
-            pltpu.VMEM((GROUP, CHUNK + 8, H), F32),
+            pltpu.VMEM((GROUP, 2 * CHUNK, H), BF16),
+            pltpu.VMEM((GROUP, 2 * CHUNK, H), BF16),
             pltpu.VMEM((2, CHUNK + 8, H), F32),
-            pltpu.VMEM((DEPTH, CHUNK + 8, H), F32),
+            pltpu.VMEM((DEPTH, 2 * CHUNK, H), BF16),
             pltpu.VMEM((BPD, BS, B), F32),
             pltpu.VMEM((BPD, 8, B), F32),
         ]

time: 52.1 us -> 50.7 us (0.973)
  Pallas kernels: 51.1 us -> 49.7 us
    pallas_call x1, Pallas kernels: 49.4 us -> 48.1 us  [shards(): pl.pallas_call(main_kernel, out_shape=(jax.ShapeDtypeStruct((BPD,), F32),...]
where the time goes in v6:
time: 50.7 us; the launch traced here: 50.5 us
  Pallas kernels  49.7 us (98%)
  between operations  0.8 us (2%)
    pallas_call x1, Pallas kernels, shards(): pl.pallas_call(main_kernel, out_shape=(jax.ShapeDtypeStruct((BPD,), F32),...  48.1 us
    pallas_call x1, Pallas kernels, shards(): pl.pallas_call(finish_kernel, out_shape=(jax.ShapeDtypeStruct((BPD,), F32...  1.65 us

profile of v6, /device:TPU:1, one launch (start us, length us, event | category | flops | bytes accessed | tf_op | source)
XLA Modules:
  0.0 50.5 jit_solution(11477585457743111369)
XLA Ops:
  0.6 48.1 %vecchia_main.1 = (f32[2]{0:T(128)}, f32[3]{0:T(128)}, f32[192,128]{1,0:T(8,128)}, bf16[256,128]{1,0:T(8,128)(2,1)}, f32[128]{0:T(128)}) custom-call(bf16[192,128]{1,0:T(8,128)(2,1)} %x_in.1, bf16[192]{0:T(256)(128)(2,1)} %resp_in.1, s32[192]{0:T(256)} %ps_in.1, bf16[128,128]{1,0:T(8,128)(2,1)} %w_in_in.1, f32[128]{0:T(128)} %b_in.1, ...), custom_call_target="tpu_custom_call" | custom-call | tf_op jit(solution)/shard_map/vecchia_main/pallas_call | solution.py:567
  48.7 1.7 %vecchia_finish.1 = (f32[2]{0:T(128)}, f32[192,128]{1,0:T(8,128)}, f32[128,128]{1,0:T(8,128)}, f32[128]{0:T(128)}, f32[128,128]{1,0:T(8,128)}, /*index=5*/f32[3]{0:T(128)}) custom-call(f32[2]{0:T(128)} %get-tuple-element.11.ll_in, f32[3]{0:T(128)} %get-tuple-element.12.hyp_in, f32[192,128]{1,0:T(8,128)} %get-tuple-element.13.grad_in, ...), custom_call_target="tpu_custom_call" | custom-call | tf_op jit(solution)/shard_map/vecchia_finish/pallas_call | solution.py:624

commit v7 on v6

--- a/solution.py
+++ b/solution.py
@@ -314,6 +314,8 @@
     mates = [
         (xs[k // 4] * 4 + ys[k % 4], (xs[k // 4] * 2 + core, ys[k % 4] * DEPTH + z)) for k in range(GROUP)
     ]
+    far = sorted(range(1, GROUP), key=lambda k: -(min(k // 4, 4 - k // 4) + min(k % 4, 4 - k % 4)))
+    deep = sorted(range(1, DEPTH), key=lambda k: -min(k, DEPTH - k))
     column = [(region, y * DEPTH + lax.rem(z + k, DEPTH)) for k in range(DEPTH)]
 
     def send(src, dst, ssem, rsem, place):
@@ -354,7 +356,7 @@
         at = pl.ds(cut.start, cut.stop - cut.start)
         return send(win_ref.at[src, at], win_ref.at[dst, at], f_send.at[sem], f_recv.at[sem], later(k))
 
-    cuts = [slice(0, 64), slice(64, 128), slice(128, ROWS + 32)]
+    cuts = [slice(0, 96), slice(96, ROWS + 32)]
     two = [shift(0, 2, cut, q, 2) for q, cut in enumerate(cuts)]
     one = shift(0, 1, slice(0, ROWS + 32), 3, 1)
 
@@ -471,7 +473,7 @@
         part[c, :CHUNK, :] = src[(c % 8) * CHUNK : (c % 8 + 1) * CHUNK]
         part[c, CHUNK:, :] = small
     copies = []
-    for k in range(1, GROUP):
+    for k in far:
         other, place = mates[k]
         copies.append(send(part.at[other], part_in.at[ga], s1.at[k], r1.at[k], place))
     part_in[ga] = part[ga]
@@ -494,7 +496,7 @@
     red_in[z, :CHUNK, :] = acc[:CHUNK].astype(BF16)
     red_in[z, CHUNK:, :] = pack(acc[CHUNK : CHUNK + 1], acc[CHUNK + 1 : CHUNK + 2])
     copies = []
-    for k in range(1, DEPTH):
+    for k in deep:
         copies.append(send(red_in.at[z], red_in.at[z], s2.at[k], r2.at[k], column[k]))
 
     @pl.when(dev >= 0)
@@ -512,7 +514,7 @@
     bsum_ref[...] = bias.reshape(H)
     place = pl.ds(pl.multiple_of(ga * CHUNK, CHUNK), CHUNK)
     copies = []
-    for k in range(1, GROUP):
+    for k in far:
         copies.append(send(mine_ref, gath.at[place], s3.at[k], r3.at[k], mates[k][1]))
     stores = [
         pltpu.make_async_copy(mine_ref, gath.at[place], out_sem.at[0]),

time: 50.7 us -> 49.6 us (0.978)
  Pallas kernels: 49.7 us -> 48.6 us
    pallas_call x1, Pallas kernels: 48.1 us -> 46.9 us  [shards(): pl.pallas_call(main_kernel, out_shape=(jax.ShapeDtypeStruct((BPD,), F32),...]
where the time goes in v7:
time: 49.6 us; the launch traced here: 49.4 us
  Pallas kernels  48.6 us (98%)
  between operations  0.8 us (2%)
    pallas_call x1, Pallas kernels, shards(): pl.pallas_call(main_kernel, out_shape=(jax.ShapeDtypeStruct((BPD,), F32),...  46.9 us
    pallas_call x1, Pallas kernels, shards(): pl.pallas_call(finish_kernel, out_shape=(jax.ShapeDtypeStruct((BPD,), F32...  1.65 us

profile of v7, /device:TPU:1, one launch (start us, length us, event | category | flops | bytes accessed | tf_op | source)
XLA Modules:
  0.0 49.4 jit_solution(9073076224718514465)
XLA Ops:
  0.6 46.9 %vecchia_main.1 = (f32[2]{0:T(128)}, f32[3]{0:T(128)}, f32[192,128]{1,0:T(8,128)}, bf16[256,128]{1,0:T(8,128)(2,1)}, f32[128]{0:T(128)}) custom-call(bf16[192,128]{1,0:T(8,128)(2,1)} %x_in.1, bf16[192]{0:T(256)(128)(2,1)} %resp_in.1, s32[192]{0:T(256)} %ps_in.1, bf16[128,128]{1,0:T(8,128)(2,1)} %w_in_in.1, f32[128]{0:T(128)} %b_in.1, ...), custom_call_target="tpu_custom_call" | custom-call | tf_op jit(solution)/shard_map/vecchia_main/pallas_call | solution.py:569
  47.6 1.7 %vecchia_finish.1 = (f32[2]{0:T(128)}, f32[192,128]{1,0:T(8,128)}, f32[128,128]{1,0:T(8,128)}, f32[128]{0:T(128)}, f32[128,128]{1,0:T(8,128)}, /*index=5*/f32[3]{0:T(128)}) custom-call(f32[2]{0:T(128)} %get-tuple-element.11.ll_in, f32[3]{0:T(128)} %get-tuple-element.12.hyp_in, f32[192,128]{1,0:T(8,128)} %get-tuple-element.13.grad_in, ...), custom_call_target="tpu_custom_call" | custom-call | tf_op jit(solution)/shard_map/vecchia_finish/pallas_call | solution.py:626

commit v8 on v7

--- a/solution.py
+++ b/solution.py
@@ -295,9 +295,9 @@
 
 def main_kernel(
     x_in, resp_in, ps_in, w_in_in, b_in, w_out_in, home_in, ids_in, cnt_in, par_in,
-    ll_ref, hyp_ref, fg_out, gath, b_out,
+    ll_out, hyp_out, fg_out, gath, b_out,
     x_ref, resp_ref, ps_ref, w_in_ref, b_ref, w_out_ref, home_ref, ids_ref, cnt_ref, par_ref,
-    fg_ref, mine_ref, bsum_ref, in_sem, out_sem,
+    ll_ref, hyp_ref, fg_ref, mine_ref, bsum_ref, in_sem, out_sem,
     win_ref, wresp_ref, feat_ref, hid_ref, dsil_ref, z_ref, e_ref, k_ref, gw_ref,
     out_buf, in_buf, part, part_in, pair, red_in, mat_ref, log_ref,
     f_send, f_recv, g_send, g_recv, s1, r1, s2, r2, s3, r3, c_send, c_recv,
@@ -520,6 +520,8 @@
         pltpu.make_async_copy(mine_ref, gath.at[place], out_sem.at[0]),
         pltpu.make_async_copy(bsum_ref, b_out, out_sem.at[1]),
         pltpu.make_async_copy(fg_ref, fg_out, out_sem.at[2]),
+        pltpu.make_async_copy(ll_ref, ll_out, out_sem.at[3]),
+        pltpu.make_async_copy(hyp_ref, hyp_out, out_sem.at[4]),
     ]
     stores[0].start()
     stores[1].start()
@@ -541,7 +543,8 @@
     perm = one_hot(ps_ref[...].reshape(1, ROWS), ROWS, 0)
     pairs = dot(perm, lanes(*split2(grad)), TN)
     fg_ref[...] = pairs[:, :H] + pairs[:, H:]
-    stores[2].start()
+    for c in stores[2:]:
+        c.start()
     for c in copies + stores:
         c.wait()
 
@@ -576,7 +579,7 @@
             jax.ShapeDtypeStruct((H,), F32),
         ),
         in_specs=[ANY] * 10,
-        out_specs=(SM, SM, ANY, ANY, ANY),
+        out_specs=(ANY,) * 5,
         scratch_shapes=[
             pltpu.VMEM((ROWS, H), BF16),
             pltpu.VMEM((ROWS,), BF16),
@@ -588,11 +591,13 @@
             pltpu.SMEM((BPD, NMAX), jnp.int32),
             pltpu.SMEM((BPD,), jnp.int32),
             pltpu.SMEM((3,), F32),
+            pltpu.SMEM((BPD,), F32),
+            pltpu.SMEM((3,), F32),
             pltpu.VMEM((ROWS, H), F32),
             pltpu.VMEM((CHUNK, H), BF16),
             pltpu.VMEM((H,), F32),
             DMA((10,)),
-            DMA((3,)),
+            DMA((5,)),
             pltpu.VMEM((WIN + 1, ROWS + 32, H), BF16),
             pltpu.VMEM(((WIN + 1) * BPD, 16, H), BF16),
             pltpu.VMEM(((WIN + 1) * BPD, BS, H), BF16),

time: 49.6 us -> 49.1 us (0.990)
  Pallas kernels: 48.6 us -> 48.1 us
where the time goes in v8:
time: 49.1 us; the launch traced here: 48.9 us
  Pallas kernels  48.1 us (98%)
  between operations  0.8 us (2%)
    pallas_call x1, Pallas kernels, shards(): pl.pallas_call(main_kernel, out_shape=(jax.ShapeDtypeStruct((BPD,), F32),...  46.4 us
    pallas_call x1, Pallas kernels, shards(): pl.pallas_call(finish_kernel, out_shape=(jax.ShapeDtypeStruct((BPD,), F32...  1.65 us

profile of v8, /device:TPU:1, one launch (start us, length us, event | category | flops | bytes accessed | tf_op | source)
XLA Modules:
  0.0 48.9 jit_solution(6944065235903207962)
XLA Ops:
  0.6 46.4 %vecchia_main.1 = (f32[2]{0:T(128)}, f32[3]{0:T(128)}, f32[192,128]{1,0:T(8,128)}, bf16[256,128]{1,0:T(8,128)(2,1)}, f32[128]{0:T(128)}) custom-call(bf16[192,128]{1,0:T(8,128)(2,1)} %x_in.1, bf16[192]{0:T(256)(128)(2,1)} %resp_in.1, s32[192]{0:T(256)} %ps_in.1, bf16[128,128]{1,0:T(8,128)(2,1)} %w_in_in.1, f32[128]{0:T(128)} %b_in.1, ...), custom_call_target="tpu_custom_call" | custom-call | tf_op jit(solution)/shard_map/vecchia_main/pallas_call | solution.py:572
  47.1 1.7 %vecchia_finish.1 = (f32[2]{0:T(128)}, f32[192,128]{1,0:T(8,128)}, f32[128,128]{1,0:T(8,128)}, f32[128]{0:T(128)}, f32[128,128]{1,0:T(8,128)}, /*index=5*/f32[3]{0:T(128)}) custom-call(f32[2]{0:T(128)} %get-tuple-element.11.ll_in, f32[3]{0:T(128)} %get-tuple-element.12.hyp_in, f32[192,128]{1,0:T(8,128)} %get-tuple-element.13.grad_in, ...), custom_call_target="tpu_custom_call" | custom-call | tf_op jit(solution)/shard_map/vecchia_finish/pallas_call | solution.py:631
